TPU v7x, 256 devices: a whole 4x4x8 slice. The times are simulated.
256 devices in a mesh: blk: 32 (over x, z_lo, core), dom: 8 (over y, z_hi).
Axes of the slice: x: 4, y: 4, z: 8 (z_hi: 2, z_lo: 4; z = z_hi * 4 + z_lo), core: 2. Of those that a mesh axis runs over, the one named last changes fastest.
Arguments:
- particles: bfloat16 [1024, 128, 128], P(('blk', 'dom')), may hold values from -8 to 8
- defocus: float32 [1024], P(('blk', 'dom')), may hold values from 290 to 3010
- noise_weight: float32 [128, 64], replicated, may hold values from 0.005 to 0.05
- projections: bfloat16 [8, 32, 128, 128], P(None, 'blk'), may hold values from -6 to 6
- row_slab: int32 [1024, 128, 1], P(('blk', 'dom')), may hold values from 0 to 31, as said below
- row_slot: int32 [1024, 128], P(('blk', 'dom')), may hold values from 0 to 511, as said below
- interp: float32 [1024, 128], P(('blk', 'dom')), may hold values from 0.25 to 1
Outputs:
- volume: float32 [8, 16384, 128], P(None, ('blk', 'dom'))
- class_weight: float32 [1024, 8], P(('blk', 'dom'))
Inputs may be any that keep to these rules, and one draw needn't show every extreme that they name: `row_slab`: the rows of one device's particles (aligned blocks of 512 rows) put at most 32 rows into one slab, and exactly 32 into some slab. Piece p of a slab holds the rows with row_slot from p * 64 to (p + 1) * 64 - 1. The rows of one device's particles put at most 4 rows into one piece of one slab, and exactly 4 into some piece.
All inputs are finite; a program needn't handle non-finite values.
Results may differ from a plain program's by a relative error of at most 0.033.
Values may be sent and summed in bfloat16 or wider, within the bound.
A program may use at most 128 MiB of HBM per device.

v0:
```python
import jax
import jax.numpy as jnp
from jax import lax
from jax.experimental import pallas as pl
from jax.experimental.pallas import tpu as pltpu
from jax.sharding import PartitionSpec as P

F32, BF16 = jnp.float32, jnp.bfloat16
MESH = pl.DeviceIdType.MESH
PI = 3.141592653589793
SIN_COEF = (
    0.9999999992267364, -0.16666665898756483, 0.008333320916259667, -0.00019840515744570079,
    2.7535452887970435e-06, -2.47248903062851e-08, 1.3598699876951359e-10,
)
SIN2_COEF = (
    0.9999999902438815, -0.3333330511544617, 0.044443119935340766, -0.00317232337316227,
    0.00013931019440764148, -3.6240280738953943e-06,
)


def reduced(angle, period, high, mid):
    turns = jnp.floor(angle * (1.0 / period) + 0.5)
    return ((angle - turns * high) - turns * mid) - turns * (period - high - mid)


def horner(coef, y):
    total = jnp.full_like(y, coef[-1])
    for c in coef[-2::-1]:
        total = total * y + c
    return total


def sine(angle):
    r = reduced(angle, 2 * PI, 6.28125, 8117 / 2**22)
    return r * horner(SIN_COEF, r * r)


def sine_squared(angle):
    r = reduced(angle, PI, 3.140625, 8117 / 2**23)
    y = r * r
    return y * horner(SIN2_COEF, y)


def iota(shape, axis):
    return lax.broadcasted_iota(jnp.int32, shape, axis)


def dot(a, b):
    return jnp.dot(a, b, preferred_element_type=F32)


def dot_nt(a, b):
    return lax.dot_general(a, b, (((1,), (1,)), ((), ())), preferred_element_type=F32)


def split_dot(values, indicator):
    high = values.astype(BF16)
    low = (values - high.astype(F32)).astype(BF16)
    return dot(high, indicator) + dot(low, indicator)


def kernel(
    part_ref, focus_ref, noise_ref, proj_ref, slab_ref, slot_ref, interp_ref,
    vol_ref, cw_ref,
    wide_p, wide_x, noise_full, cols, weight_in, proj_in, focus_in, rows_ins,
    left_op, right_op, score, turn_tab, hop1_out, hop1_in, hop2_out, hop2_in, stat, cwt, cw_flat, coef_tab,
    w_send, w_recv, p_send, p_recv, f_send, f_recv, h1_send, h1_recv, h2_send, h2_recv,
    s_send, s_recv, c_send, c_recv,
):
    blk, dom = lax.axis_index("blk"), lax.axis_index("dom")
    x, a = blk // 8, blk % 8
    z, core = a // 2, a % 2
    g = x * 8 + dom

    def copy(src, dst, send, recv, to_blk, to_dom):
        return pltpu.make_async_remote_copy(
            src_ref=src, dst_ref=dst, send_sem=send, recv_sem=recv,
            device_id=(to_blk, to_dom), device_id_type=MESH,
        )

    def a_peer(i):
        return (a + i) % 8

    def g_peer(i):
        return (g + i) % 32

    barrier = pltpu.get_barrier_semaphore()

    def greet_a(i, _):
        pl.semaphore_signal(barrier, inc=1, device_id=(x * 8 + a_peer(i), dom), device_id_type=MESH)
        return 0

    def greet_g(i, _):
        to = g_peer(i)
        pl.semaphore_signal(barrier, inc=1, device_id=((to // 8) * 8 + a, to % 8), device_id_type=MESH)
        return 0

    lax.fori_loop(1, 8, greet_a, 0)
    lax.fori_loop(1, 32, greet_g, 0)

    wide_x[...] = proj_ref[...].astype(F32)

    def order_proj(q, _):
        tile = wide_x[pl.ds(q, 16, stride=64), :].astype(BF16)
        proj_in[x, pl.ds(pl.multiple_of(q * 16, 16), 16), :] = tile
        return 0

    lax.fori_loop(0, 64, order_proj, 0, unroll=4)

    pl.semaphore_wait(barrier, 38)

    right, left = ((x + 1) % 4) * 8 + a, ((x + 3) % 4) * 8 + a
    top, low = pl.ds(0, 512), pl.ds(512, 512)

    def p_copy(k, block, half, to):
        return copy(proj_in.at[block, half], proj_in.at[block, half], p_send.at[k], p_recv.at[k], to, dom)

    p_copy(0, x, top, right).start()
    p_copy(2, x, low, left).start()
    p_copy(1, x, low, right).start()
    p_copy(3, x, top, left).start()

    focus_in[a] = focus_ref[...]

    def f_copy(i):
        return copy(focus_in.at[a], focus_in.at[a], f_send.at[i], f_recv.at[i], x * 8 + a_peer(i), dom)

    lax.fori_loop(1, 8, lambda i, _: (f_copy(i).start(), 0)[1], 0)

    noise_full[...] = jnp.concatenate([noise_ref[...], noise_ref[...]], axis=1)
    interp = interp_ref[...]
    for p in range(4):
        cols[p * 128:(p + 1) * 128, :] = jnp.broadcast_to(interp[p:p + 1, :], (128, 128)).T
    wide_p[...] = part_ref[...].astype(F32)
    lane8 = iota((8, 128), 1)
    kx = (lane8 % 64).astype(F32)
    kx2 = kx * kx
    odd8 = (iota((8, 128), 0) % 2) == 1
    half8 = lane8 < 64
    focus = focus_ref[...]

    def weigh(q2, _):
        tiles = []
        for h in range(2):
            q = q2 * 2 + h
            rows = pl.ds(q, 8, stride=64)
            image = wide_p[rows, :]
            ky = jnp.where(odd8, q - 64, q).astype(F32)
            radius = (kx2 + ky * ky) * (1.0 / 16384.0)
            signal = -sine(focus * radius + 0.1) * image
            noise = jnp.where(odd8, noise_full[pl.ds(q + 64, 1), :], noise_full[pl.ds(q, 1), :])
            tiles.append(signal * noise)
            rows_ins[rows, :] = signal * cols[rows, :]
        weight_in[a, pl.ds(pl.multiple_of(q2 * 16, 16), 16), :] = jnp.concatenate(tiles, axis=0).astype(BF16)
        return 0

    lax.fori_loop(0, 32, weigh, 0, unroll=2)

    def w_copy(k, block, to):
        return copy(weight_in.at[block], weight_in.at[block], w_send.at[k], w_recv.at[k], x * 8 + to, dom)

    for i in range(1, 4):
        w_copy(i, a, ((z + i) % 4) * 2 + core).start()
    w_copy(0, a, z * 2 + 1 - core).start()

    slab, slot = slab_ref[...], slot_ref[...]
    piece = slot // 64
    bucket = (slab * 8 + piece).astype(F32)
    earlier = iota((128, 128), 0) < iota((128, 128), 1)
    ranks = []
    across = [jnp.broadcast_to(bucket[p:p + 1, :], (128, 128)) for p in range(4)]
    down = [b.T for b in across]
    for p in range(4):
        rank = jnp.zeros((1, 128), F32)
        for p2 in range(p + 1):
            same = across[p] == down[p2]
            if p2 == p:
                same = same & earlier
            rank = rank + jnp.sum(jnp.where(same, 1.0, 0.0), axis=0, keepdims=True)
        ranks.append(rank)
    base = (((slab // 8) * 8 + piece) * 32 + (slab % 8) * 4).astype(F32)
    position = [base[p:p + 1, :] + ranks[p] for p in range(4)]
    key4 = ((slot % 64) * 4 + iota((4, 128), 0) + 1).astype(F32)
    keys = jnp.concatenate([key4[p:p + 1, :] for p in range(4)], axis=1)
    keys16 = jnp.broadcast_to(keys, (16, 512)).astype(BF16)
    mine16 = iota((16, 128), 0) == g % 16
    ins = rows_ins[...].astype(BF16)
    slot_iota = iota((128, 128), 0).astype(F32)

    def dispatch(chunk, _):
        where = slot_iota + (chunk * 128).astype(F32)
        pick = jnp.concatenate([jnp.where(where == position[p], 1.0, 0.0) for p in range(4)], axis=1).astype(BF16)
        data = dot(pick, ins).astype(BF16)
        meta = jnp.where(mine16, dot_nt(keys16, pick), 0.0).astype(BF16)
        for t in range(4):
            hop1_out[chunk * 4 + t, 0:32, :] = data[t * 32:(t + 1) * 32]
            hop1_out[chunk * 4 + t, 32:48, :] = meta
        return 0

    lax.fori_loop(0, 8, dispatch, 0)

    def h1_copy(i):
        to = g_peer(i)
        return copy(hop1_out.at[to], hop1_in.at[g], h1_send.at[i], h1_recv.at[i], (to // 8) * 8 + a, to % 8)

    lax.fori_loop(1, 32, lambda i, _: (h1_copy(i).start(), 0)[1], 0)
    hop1_in[g] = hop1_out[g]

    lax.fori_loop(1, 8, lambda i, _: (f_copy(i).wait_recv(), 0)[1], 0)

    def norms(q, _):
        q_hi = q + 32
        ky = jnp.where(odd8, -64, 0) + jnp.where(half8, q, q_hi)
        kyf = ky.astype(F32)
        radius = (kx2 + kyf * kyf) * (1.0 / 16384.0)
        n_lo = jnp.where(odd8, noise_full[pl.ds(q + 64, 1), :], noise_full[pl.ds(q, 1), :])
        n_hi = jnp.where(odd8, noise_full[pl.ds(q_hi + 64, 1), :], noise_full[pl.ds(q_hi, 1), :])
        outs_lo, outs_hi = [], []
        for b in range(8):
            squared = sine_squared(focus_in[b] * radius + 0.1)
            turned = pltpu.roll(squared, 64, 1)
            outs_lo.append(jnp.where(half8, squared, turned) * n_lo)
            outs_hi.append(jnp.where(half8, turned, squared) * n_hi)
        left_op[q, 192:256, 0:128] = jnp.concatenate(outs_lo, axis=0).astype(BF16)
        left_op[q, 192:256, 128:256] = jnp.concatenate(outs_hi, axis=0).astype(BF16)
        return 0

    lax.fori_loop(0, 32, norms, 0)

    lane16 = iota((16, 128), 1)
    angle_x = (lane16 % 64).astype(F32) * (2.0 * PI / 128.0)
    cos_x = sine(angle_x + 0.5 * PI)
    sin_x = sine(angle_x) * jnp.where(lane16 < 64, 1.0, -1.0)
    angle_y = iota((64, 128), 0).astype(F32) * (2.0 * PI / 128.0)
    turn_tab[0] = sine(angle_y + 0.5 * PI)
    turn_tab[1] = sine(angle_y) * jnp.where(iota((64, 128), 1) < 64, -1.0, 1.0)
    flip16 = jnp.where(iota((16, 128), 0) % 2 == 1, -1.0, 1.0)

    def views(block, begin, end):
        row = pl.multiple_of(block * 16, 16)

        def step(q, _):
            for h in range(2):
                qq = q + 32 * h
                image = proj_in[block, pl.ds(pl.multiple_of(qq * 16, 16), 16), :].astype(F32)
                lanes = pl.ds(h * 128, 128)
                u = image * (flip16 * turn_tab[0, pl.ds(qq, 1), :])
                v = pltpu.roll(image, 64, 1) * (flip16 * turn_tab[1, pl.ds(qq, 1), :])
                right_op[q, pl.ds(row, 16), lanes] = (u - v).astype(BF16)
                right_op[q, pl.ds(row + 64, 16), lanes] = image.astype(BF16)
                right_op[q, pl.ds(row + 128, 16), lanes] = (u + v).astype(BF16)
                right_op[q, pl.ds(row + 192, 16), lanes] = (image * image).astype(BF16)
            return 0

        lax.fori_loop(begin, end, step, 0, unroll=2)

    def turns(zz):
        row = pl.multiple_of(zz * 16, 16)

        def step(q2, _):
            for h in range(2):
                at = pl.ds(pl.multiple_of((q2 + 16 * h) * 16, 16), 16)
                first = weight_in[zz * 2, at, :].astype(F32)
                second = weight_in[zz * 2 + 1, at, :].astype(F32)
                lanes = pl.ds(h * 128, 128)
                for e in range(2):
                    image = jnp.concatenate([first[e * 8:e * 8 + 8], second[e * 8:e * 8 + 8]], axis=0)
                    u = image * cos_x
                    v = pltpu.roll(image, 64, 1) * sin_x
                    left_op[q2 * 2 + e, pl.ds(row, 16), lanes] = (u - v).astype(BF16)
                    left_op[q2 * 2 + e, pl.ds(row + 64, 16), lanes] = image.astype(BF16)
                    left_op[q2 * 2 + e, pl.ds(row + 128, 16), lanes] = (u + v).astype(BF16)
            return 0

        lax.fori_loop(0, 16, step, 0)

    from_left, from_right, across_x = (x + 3) % 4, (x + 1) % 4, (x + 2) % 4

    p_copy(0, from_left, top, right).wait_recv()
    p_copy(4, from_left, top, right).start()
    p_copy(2, from_right, low, left).wait_recv()
    p_copy(5, from_right, low, left).start()
    views(x, 0, 32)
    for i in (1, 3, 2):
        block = ((z + 4 - i) % 4) * 2 + core
        w_copy(i, block, a).wait_recv()
        w_copy(3 + i, block, z * 2 + 1 - core).start()
    w_copy(0, a, a).wait_recv()
    turns(z)
    p_copy(1, from_left, low, right).wait_recv()
    views(from_left, 0, 32)
    p_copy(3, from_right, top, left).wait_recv()
    views(from_right, 0, 32)

    lax.fori_loop(1, 32, lambda i, _: (h1_copy(i).wait_recv(), 0)[1], 0)
    o_row, o_col = iota((128, 128), 0), iota((128, 128), 1)
    mix = jnp.where(o_col == ((o_row // 4) % 4) * 32 + (o_row // 16) * 4 + o_row % 4, 1.0, 0.0).astype(BF16)

    def regroup(group, _):
        four = jnp.concatenate([hop1_in[group * 4 + t, 0:32, :] for t in range(4)], axis=0)
        mixed = dot(mix, four).astype(BF16)
        at = pl.ds(pl.multiple_of(group * 16, 16), 16)
        for b in range(8):
            hop2_out[b, at, :] = mixed[b * 16:(b + 1) * 16]
        return 0

    lax.fori_loop(0, 8, regroup, 0)
    key_rows = []
    for half in range(2):
        total = hop1_in[half * 16, 32:48, :].astype(F32)
        for t in range(1, 16):
            total = total + hop1_in[half * 16 + t, 32:48, :].astype(F32)
        key_rows.append(total)
    meta = jnp.concatenate(key_rows, axis=0).astype(BF16)
    for b in range(8):
        hop2_out[b, 128:160, :] = meta

    def h2_copy(i):
        to = a_peer(i)
        return copy(hop2_out.at[to], hop2_in.at[a], h2_send.at[i], h2_recv.at[i], x * 8 + to, dom)

    lax.fori_loop(1, 8, lambda i, _: (h2_copy(i).start(), 0)[1], 0)
    hop2_in[a] = hop2_out[a]

    for i in (1, 3, 2):
        block = ((z + 4 - i) % 4) * 2 + 1 - core
        w_copy(3 + i, block, a).wait_recv()
        turns((z + 4 - i) % 4)
    p_copy(4, across_x, top, right).wait_recv()
    p_copy(5, across_x, low, left).wait_recv()
    views(across_x, 0, 32)

    score[...] = jnp.zeros_like(score)

    def multiply(k, _):
        part = dot_nt(left_op[k], right_op[k])
        score[0] += part[:, 0:128]
        score[1] += part[:, 128:256]
        return 0

    lax.fori_loop(0, 32, multiply, 0, unroll=4)

    even = jnp.concatenate([score[h, pl.ds(0, 128, stride=2), :] for h in range(2)], axis=1)
    odd = jnp.concatenate([score[h, pl.ds(1, 128, stride=2), :] for h in range(2)], axis=1)
    folded = even + pltpu.roll(odd, 255, 1)
    lane32 = iota((32, 128), 1)
    penalty = folded[96:128, 128:256]
    penalty = 0.5 * jnp.where(lane32 < 64, pltpu.roll(penalty, 64, 1), penalty)
    penalty = jnp.concatenate([penalty, penalty], axis=1)
    lane = iota((32, 256), 1)
    valid = (lane % 2 == 0) & (lane < 192)
    scores = [jnp.where(valid, folded[s * 32:(s + 1) * 32, :] - penalty, -3e38) for s in range(3)]
    top_score = jnp.max(jnp.maximum(jnp.maximum(scores[0], scores[1]), scores[2]), axis=1, keepdims=True)
    weight = sum(jnp.where(valid, jnp.exp(s - top_score), 0.0) for s in scores)
    t_row, t_col = iota((256, 256), 0), iota((256, 256), 1)
    same_class = jnp.where((t_row // 2) % 8 == t_col % 8, 1.0, 0.0).astype(BF16)
    own = lane // 8 == iota((32, 256), 0)
    sums = jnp.sum(jnp.where(own, split_dot(weight, same_class), 0.0), axis=0, keepdims=True)
    tops = jnp.sum(jnp.where(own, top_score, 0.0), axis=0, keepdims=True)
    row8 = iota((8, 128), 0)
    tile = jnp.where(row8 == 0, sums[:, 0:128], 0.0)
    tile = jnp.where(row8 == 1, sums[:, 128:256], tile)
    tile = jnp.where(row8 == 2, tops[:, 0:128], tile)
    stat[a] = jnp.where(row8 == 3, tops[:, 128:256], tile)

    def s_copy(i):
        return copy(stat.at[a], stat.at[a], s_send.at[i], s_recv.at[i], x * 8 + a_peer(i), dom)

    lax.fori_loop(1, 8, lambda i, _: (s_copy(i).start(), 0)[1], 0)
    lax.fori_loop(1, 8, lambda i, _: (s_copy(i).wait_recv(), 0)[1], 0)
    best = stat[0]
    for b in range(1, 8):
        best = jnp.maximum(best, stat[b])
    total = jnp.zeros((8, 128), F32)
    for b in range(8):
        tile = stat[b]
        total = total + tile * pltpu.roll(jnp.exp(tile - best), 6, 0)
    total = jnp.where(row8 < 2, total, 0.0)
    same_particle = jnp.where(o_row // 8 == o_col // 8, 1.0, 0.0).astype(BF16)
    class_w = jnp.where(row8 < 2, total / split_dot(total, same_particle), 0.0)
    first, second = class_w[0:1, :], class_w[1:2, :]
    tile = jnp.where(row8 == (g % 4) * 2, first, 0.0)
    cwt[g] = jnp.where(row8 == (g % 4) * 2 + 1, second, tile)

    def c_copy(i):
        to = g_peer(i)
        return copy(cwt.at[g], cwt.at[g], c_send.at[i], c_recv.at[i], (to // 8) * 8 + a, to % 8)

    lax.fori_loop(1, 32, lambda i, _: (c_copy(i).start(), 0)[1], 0)

    flat = jnp.concatenate([first, second], axis=1)
    spread = jnp.where(iota((8, 256), 1) // 8 == iota((8, 256), 0) + a * 4, flat, 0.0)
    gather_class = jnp.where(iota((256, 128), 0) % 8 == iota((256, 128), 1), 1.0, 0.0).astype(BF16)
    hi = spread.astype(BF16)
    rest = spread - hi.astype(F32)
    cw_flat[...] = dot(hi, gather_class) + split_dot(rest, gather_class)
    cw_ref[...] = cw_flat[0:4, 0:8]

    lax.fori_loop(1, 8, lambda i, _: (h2_copy(i).wait_recv(), 0)[1], 0)
    lax.fori_loop(1, 32, lambda i, _: (c_copy(i).wait_recv(), 0)[1], 0)

    gathered = []
    for group in range(8):
        tile = cwt[group * 4]
        for t in range(1, 4):
            tile = tile + cwt[group * 4 + t]
        gathered.append(tile)
    table = jnp.concatenate(gathered + [jnp.zeros((64, 128), F32)], axis=0).T.astype(BF16)
    for half in range(2):
        repeat = jnp.where(o_row == (o_col // 4) * 2 + half, 1.0, 0.0).astype(BF16)
        coef_tab[half * 128:(half + 1) * 128, :] = dot(table, repeat)
    pick_key = jnp.where(o_row == (g % 4) * 32 + a * 4 + o_col % 4, 1.0, 0.0).astype(BF16)
    own_source = lane32 // 4 == iota((32, 128), 0)
    slot64 = iota((64, 128), 0).astype(F32)
    vol_ref[...] = jnp.zeros_like(vol_ref)

    def insert(pair, _):
        parts = []
        for h in range(2):
            source = pair * 2 + h
            keys_of = dot(hop2_in[source, 128:160, :], pick_key)
            key = jnp.sum(jnp.where(own_source, keys_of, 0.0), axis=0, keepdims=True) - 1.0
            at_slot = jnp.floor(key * 0.25)
            which = key - 4.0 * at_slot
            coef = jnp.zeros((8, 128), F32)
            for p in range(4):
                rows = pl.ds(pl.multiple_of(source * 32 + p * 8, 8), 8)
                coef = jnp.where(which == float(p), coef_tab[rows, :], coef)
            hit = slot64 == at_slot
            parts.append(
                jnp.concatenate([jnp.where(hit, coef[c:c + 1, :], 0.0) for c in range(8)], axis=0).astype(BF16)
            )
        rows_in = jnp.concatenate([hop2_in[pair * 2, 0:128, :], hop2_in[pair * 2 + 1, 0:128, :]], axis=0)
        vol_ref[...] += dot(jnp.concatenate(parts, axis=1), rows_in)
        return 0

    lax.fori_loop(0, 4, insert, 0)

    for k in range(6):
        p_copy(k, x, top, right).wait_send()
    for k in range(7):
        w_copy(k, a, a).wait_send()
    lax.fori_loop(1, 8, lambda i, _: (f_copy(i).wait_send(), h2_copy(i).wait_send(), s_copy(i).wait_send(), 0)[3], 0)
    lax.fori_loop(1, 32, lambda i, _: (h1_copy(i).wait_send(), c_copy(i).wait_send(), 0)[2], 0)


def per_device(particles, defocus, noise_weight, projections, row_slab, row_slot, interp):
    vmem, dma = pltpu.VMEM, pltpu.SemaphoreType.DMA
    focus = jnp.broadcast_to(jnp.repeat(defocus, 2)[:, None], (8, 128))
    volume, class_weight = pl.pallas_call(
        kernel,
        out_shape=(jax.ShapeDtypeStruct((512, 128), F32), jax.ShapeDtypeStruct((4, 8), F32)),
        in_specs=[pl.BlockSpec(memory_space=vmem)] * 7,
        out_specs=(pl.BlockSpec(memory_space=vmem), pl.BlockSpec(memory_space=vmem)),
        scratch_shapes=[
            vmem((512, 128), F32),
            vmem((1024, 128), F32),
            vmem((128, 128), F32),
            vmem((512, 128), F32),
            vmem((8, 512, 128), BF16),
            vmem((4, 1024, 128), BF16),
            vmem((8, 8, 128), F32),
            vmem((512, 128), F32),
            vmem((32, 256, 256), BF16),
            vmem((32, 256, 256), BF16),
            vmem((2, 256, 128), F32),
            vmem((2, 64, 128), F32),
            vmem((32, 48, 128), BF16),
            vmem((32, 48, 128), BF16),
            vmem((8, 160, 128), BF16),
            vmem((8, 160, 128), BF16),
            vmem((8, 8, 128), F32),
            vmem((32, 8, 128), F32),
            vmem((8, 128), F32),
            vmem((256, 128), F32),
            dma((7,)), dma((7,)), dma((6,)), dma((6,)), dma((8,)), dma((8,)), dma((32,)), dma((32,)),
            dma((8,)), dma((8,)), dma((8,)), dma((8,)), dma((32,)), dma((32,)),
        ],
        compiler_params=pltpu.CompilerParams(
            collective_id=0, has_side_effects=True, vmem_limit_bytes=40 * 1024 * 1024
        ),
    )(
        particles.reshape(512, 128), focus, noise_weight, projections.reshape(1024, 128),
        row_slab.reshape(4, 128), row_slot, interp,
    )
    return volume.reshape(8, 64, 128), class_weight


def solution(mesh):
    in_specs = (
        P(("blk", "dom"), None, None),
        P(("blk", "dom")),
        P(),
        P(None, "blk", None, None),
        P(("blk", "dom"), None, None),
        P(("blk", "dom"), None),
        P(("blk", "dom"), None),
    )
    out_specs = (P(None, ("blk", "dom"), None), P(("blk", "dom"), None))
    return jax.shard_map(per_device, mesh=mesh, in_specs=in_specs, out_specs=out_specs, check_vma=False)
```

profile of v0, /device:TPU:1, one launch (start us, length us, event | category | flops | bytes accessed | tf_op | source)
XLA Modules:
  0.0 67.1 jit_solution(2660332308366483176)
XLA Ops:
  0.6 0.0 copy-start.5
  0.6 0.6 copy-done.5
  1.3 0.1 broadcast_in_dim.10
  1.4 0.1 broadcast_in_dim.11
  1.4 0.1 broadcast_in_dim.12.focus_ref
  1.5 0.0 copy-start.2
  1.5 0.0 copy-start.3
  1.5 0.0 copy-start.4
  1.5 0.9 %copy.10.noise_ref = f32[128,64]{1,0:T(8,128)S(1)} copy(f32[128,64]{0,1:T(8,128)} %param.9) | data formatting | bytes 65536 | tf_op args[2]
  2.4 0.0 copy-done.2
  2.4 0.0 copy-done.3
  2.4 0.0 copy-done.4
  2.4 0.0 copy-start
  2.5 0.9 %copy-done = bf16[8,1,128,128]{3,2,1,0:T(8,128)(2,1)S(1)} copy-done((bf16[8,1,128,128]{3,2,1,0:T(8,128)(2,1)S(1)}, bf16[8,1,128,128]{3,2,1,0:T(8,128)(2,1)}, u32[]{:S(2)}) %copy-start) | copy-done | bytes 262168
  3.4 0.0 copy-start.1
  3.4 0.9 %copy-done.1 = bf16[4,128,128]{2,1,0:T(8,128)(2,1)S(1)} copy-done((bf16[4,128,128]{2,1,0:T(8,128)(2,1)S(1)}, bf16[4,128,128]{2,1,0:T(8,128)(2,1)}, u32[]{:S(2)}) %copy-start.1) | copy-done | bytes 131096
  4.3 61.5 %shard_map.86 = (f32[512,128]{1,0:T(8,128)S(1)}, f32[4,8]{1,0:T(4,128)S(1)}) custom-call(bf16[512,128]{1,0:T(8,128)(2,1)S(1)} %bitcast.6, f32[8,128]{1,0:T(8,128)S(1)} %broadcast_in_dim.12.focus_ref, f32[128,64]{1,0:T(8,128)S(1)} %copy.10.noise_ref, bf16[1024,128]{1,0:T(8,128)(2,1)S(1)} %bitcast.4, s32[4,128]{1,0:T(4,128)S(1)} %bitcast.7, ...), custom_call_target="tpu_custom_call" | custom-call | tf_op jit(solution)/shard_map/pallas_call | solution.py:450
  65.9 0.7 %copy.13 = f32[8,64,128]{2,1,0:T(8,128)} copy(f32[8,64,128]{2,1,0:T(8,128)S(1)} %bitcast.5) | data formatting | bytes 524288
  66.6 0.6 copy.14
Async XLA Ops:
  0.6 0.7 copy-start.5
  1.5 0.9 %copy-start.2 = (s32[4,128,1]{1,2,0:T(1,128)S(1)}, s32[4,128,1]{1,2,0:T(1,128)}, u32[]{:S(2)}) copy-start(s32[4,128,1]{1,2,0:T(1,128)} %param.11) | copy-start | bytes 6148
  1.5 0.9 %copy-start.3 = (s32[4,128]{1,0:T(4,128)S(1)}, s32[4,128]{1,0:T(4,128)}, u32[]{:S(2)}) copy-start(s32[4,128]{1,0:T(4,128)} %slot_ref.1) | copy-start | bytes 6148
  1.5 0.9 %copy-start.4 = (f32[4,128]{1,0:T(4,128)S(1)}, f32[4,128]{1,0:T(4,128)}, u32[]{:S(2)}) copy-start(f32[4,128]{1,0:T(4,128)} %interp_ref.1) | copy-start | bytes 6148
  2.4 1.0 %copy-start = (bf16[8,1,128,128]{3,2,1,0:T(8,128)(2,1)S(1)}, bf16[8,1,128,128]{3,2,1,0:T(8,128)(2,1)}, u32[]{:S(2)}) copy-start(bf16[8,1,128,128]{3,2,1,0:T(8,128)(2,1)} %param.10) | copy-start | bytes 786436
  3.4 0.9 %copy-start.1 = (bf16[4,128,128]{2,1,0:T(8,128)(2,1)S(1)}, bf16[4,128,128]{2,1,0:T(8,128)(2,1)}, u32[]{:S(2)}) copy-start(bf16[4,128,128]{2,1,0:T(8,128)(2,1)} %param.7) | copy-start | bytes 393220
where the time goes:
time: 67.4 us; the launch traced here: 67.1 us
  Pallas kernels  61.5 us (91%)
  local copies, waits for them, and re-layouts  4.91 us (7%)
  between operations  0.69 us (1%)
    pallas_call x1, Pallas kernels, per_device(): pl.pallas_call(kernel, out_shape=(jax.ShapeDtypeStruct((512, 128), F32),...  61.5 us
    unnamed x15, local copies, waits for them, and re-layouts  4.68 us

commit v1 on v0

v1 whole, which is shorter than its diff:
```python
import jax
import jax.numpy as jnp
from jax import lax
from jax.experimental import pallas as pl
from jax.experimental.pallas import tpu as pltpu
from jax.sharding import PartitionSpec as P

F32, BF16 = jnp.float32, jnp.bfloat16
MESH = pl.DeviceIdType.MESH
PI = 3.141592653589793
SIN_COEF = (
    0.9999999992267364, -0.16666665898756483, 0.008333320916259667, -0.00019840515744570079,
    2.7535452887970435e-06, -2.47248903062851e-08, 1.3598699876951359e-10,
)
SIN2_COEF = (
    0.9999999902438815, -0.3333330511544617, 0.044443119935340766, -0.00317232337316227,
    0.00013931019440764148, -3.6240280738953943e-06,
)


def reduced(angle, period, high, mid):
    turns = jnp.floor(angle * (1.0 / period) + 0.5)
    return ((angle - turns * high) - turns * mid) - turns * (period - high - mid)


def horner(coef, y):
    total = jnp.full_like(y, coef[-1])
    for c in coef[-2::-1]:
        total = total * y + c
    return total


def sine(angle):
    r = reduced(angle, 2 * PI, 6.28125, 8117 / 2**22)
    return r * horner(SIN_COEF, r * r)


def sine_squared(angle):
    r = reduced(angle, PI, 3.140625, 8117 / 2**23)
    y = r * r
    return y * horner(SIN2_COEF, y)


def iota(shape, axis):
    return lax.broadcasted_iota(jnp.int32, shape, axis)


def dot(a, b):
    return jnp.dot(a, b, preferred_element_type=F32)


def dot_nt(a, b):
    return lax.dot_general(a, b, (((1,), (1,)), ((), ())), preferred_element_type=F32)


def split_dot(values, indicator):
    high = values.astype(BF16)
    low = (values - high.astype(F32)).astype(BF16)
    return dot(high, indicator) + dot(low, indicator)


def kernel(
    part_hbm, focus_hbm, noise_hbm, proj_hbm, slab_hbm, slot_hbm, interp_hbm,
    vol_ref, cw_ref,
    part_ref, focus_ref, noise_ref, proj_ref, slab_ref, slot_ref, interp_ref,
    wide_p, wide_x, noise_full, cols, weight_in, proj_in, focus_in, rows_ins,
    left_op, right_op, score, turn_tab, hop1_out, hop1_in, hop2_out, hop2_in, stat, cwt, cw_flat, coef_tab,
    in_sem, w_send, w_recv, t_send, t_recv, p_send, p_recv, f_send, f_recv, h1_send, h1_recv, h2_send, h2_recv,
    s_send, s_recv, c_send, c_recv,
):
    blk, dom = lax.axis_index("blk"), lax.axis_index("dom")
    x, a = blk // 8, blk % 8
    z, core = a // 2, a % 2
    y, z_hi = dom // 2, dom % 2
    u = x * 4 + y
    v = z_hi * 8 + a
    g = z_hi * 16 + u

    def copy(src, dst, send, recv, to_blk, to_dom):
        return pltpu.make_async_remote_copy(
            src_ref=src, dst_ref=dst, send_sem=send, recv_sem=recv,
            device_id=(to_blk, to_dom), device_id_type=MESH,
        )

    def fetch(k, src, dst):
        return pltpu.make_async_copy(src, dst, in_sem.at[k])

    fetches = [
        fetch(0, part_hbm, part_ref), fetch(1, focus_hbm, focus_ref), fetch(2, noise_hbm, noise_ref),
        fetch(3, interp_hbm, interp_ref), fetch(4, proj_hbm, proj_ref), fetch(5, slab_hbm, slab_ref),
        fetch(6, slot_hbm, slot_ref),
    ]
    for f in fetches:
        f.start()

    def alpha(i):
        return x * 8 + (a + i) % 8, dom

    def gamma(i):
        to = (g + i) % 32
        return ((to % 16) // 4) * 8 + a, (to % 4) * 2 + to // 16

    def plane(i):
        to = (u + i) % 16
        return (to // 4) * 8 + a, (to % 4) * 2 + z_hi

    def column(i):
        to = (v + i) % 16
        return x * 8 + to % 8, y * 2 + to // 8

    barrier = pltpu.get_barrier_semaphore()

    def greet(who):
        def send(i, _):
            pl.semaphore_signal(barrier, inc=1, device_id=who(i), device_id_type=MESH)
            return 0
        return send

    lax.fori_loop(1, 16, greet(column), 0)
    lax.fori_loop(1, 32, greet(gamma), 0)

    def p_copy(k, block, part, to):
        rows = pl.ds(part * 256, 256)
        return copy(proj_in.at[block, rows], proj_in.at[block, rows], p_send.at[k], p_recv.at[k], to, dom)

    def w_copy(k, block, half, to):
        rows = pl.ds(half * 256, 256)
        return copy(
            weight_in.at[block, rows], weight_in.at[block, rows], w_send.at[k * 2 + half],
            w_recv.at[(block // 2) * 2 + half], x * 8 + to, dom,
        )

    def t_copy(block, half):
        rows = pl.ds(half * 256, 256)
        k = (block // 2) * 2 + half
        return copy(
            weight_in.at[block, rows], weight_in.at[block, rows], t_send.at[k], t_recv.at[k],
            x * 8 + z * 2 + 1 - core, dom,
        )

    right, left = ((x + 1) % 4) * 8 + a, ((x + 3) % 4) * 8 + a
    from_left, from_right, across_x = (x + 3) % 4, (x + 1) % 4, (x + 2) % 4

    def to_right(part):
        return p_copy(part, x, part, right)

    def to_left(part):
        return p_copy(4 + part, x, part, left)

    def came_left(part):
        return p_copy(part, from_left, part, right)

    def came_right(part):
        return p_copy(4 + part, from_right, part, left)

    def pass_right(part):
        return p_copy(8 + part, from_left, part, right)

    def pass_left(part):
        return p_copy(8 + part, from_right, part, left)

    def came_across(part):
        return p_copy(8 + part, across_x, part, right)

    def each_z(act):
        for away in (2, 1):
            for sign in (1, -1):
                target = z + sign * away

                @pl.when((target >= 0) & (target < 4))
                def _():
                    act(target)

    relays = (z == 1) | (z == 2)
    relay_from, relay_to = (2 - z) * 3, (z - 1) * 3

    lane8 = iota((8, 128), 1)
    row8 = iota((8, 128), 0)
    kx = (lane8 % 64).astype(F32)
    kx2 = kx * kx
    odd8 = (row8 % 2) == 1
    half8 = lane8 < 64

    for k in (1, 2, 3):
        fetches[k].wait()
    noise_half = noise_ref[...]
    noise_full[...] = jnp.concatenate([noise_half, noise_half], axis=0).T
    interp = interp_ref[...]
    for p in range(4):
        cols[p * 128:(p + 1) * 128, :] = jnp.broadcast_to(interp[p:p + 1, :], (128, 128)).T
    lane4 = iota((8, 4), 1)
    focus4 = jnp.broadcast_to(focus_ref[...], (8, 4))
    focus = jnp.sum(jnp.where(lane4 == iota((8, 4), 0) // 2, focus4, 0.0), axis=1, keepdims=True)
    focus = jnp.broadcast_to(focus, (8, 128))
    focus_in[a] = focus
    fetches[0].wait()
    wide_p[...] = part_ref[...].astype(F32)

    def weigh(q2, _):
        tiles = []
        for h in range(2):
            q = q2 * 2 + h
            rows = pl.ds(q, 8, stride=64)
            image = wide_p[rows, :]
            ky = jnp.where(odd8, q - 64, q).astype(F32)
            radius = (kx2 + ky * ky) * (1.0 / 16384.0)
            signal = -sine(focus * radius + 0.1) * image
            noise = jnp.where(odd8, noise_full[pl.ds(q + 64, 1), :], noise_full[pl.ds(q, 1), :])
            tiles.append(signal * noise)
            rows_ins[rows, :] = signal * cols[rows, :]
        weight_in[a, pl.ds(pl.multiple_of(q2 * 16, 16), 16), :] = jnp.concatenate(tiles, axis=0).astype(BF16)
        return 0

    def order_proj(q, _):
        tile = wide_x[pl.ds(q, 16, stride=64), :].astype(BF16)
        proj_in[x, pl.ds(pl.multiple_of(q * 16, 16), 16), :] = tile
        return 0

    def f_copy(i):
        to = alpha(i)
        return copy(focus_in.at[a], focus_in.at[a], f_send.at[i], f_recv.at[i], to[0], to[1])

    lax.fori_loop(0, 16, weigh, 0, unroll=4)
    pl.semaphore_wait(barrier, 46)
    each_z(lambda target: w_copy(target, a, 0, target * 2 + core).start())
    t_copy(a, 0).start()
    fetches[4].wait()
    wide_x[...] = proj_ref[...].astype(F32)
    lax.fori_loop(0, 32, order_proj, 0, unroll=8)
    to_right(0).start()
    to_left(1).start()
    to_right(1).start()
    to_left(0).start()
    lax.fori_loop(1, 8, lambda i, _: (f_copy(i).start(), 0)[1], 0)
    lax.fori_loop(16, 32, weigh, 0, unroll=4)
    each_z(lambda target: w_copy(target, a, 1, target * 2 + core).start())
    t_copy(a, 1).start()
    lax.fori_loop(32, 64, order_proj, 0, unroll=8)
    to_right(2).start()
    to_left(3).start()
    to_right(3).start()
    to_left(2).start()

    fetches[5].wait()
    fetches[6].wait()
    slab, slot = slab_ref[...], slot_ref[...]
    piece = slot // 64
    bucket = (slab * 8 + piece).astype(F32)
    earlier = iota((128, 128), 0) < iota((128, 128), 1)
    ranks = []
    across = [jnp.broadcast_to(bucket[p:p + 1, :], (128, 128)) for p in range(4)]
    down = [b.T for b in across]
    for p in range(4):
        rank = jnp.zeros((1, 128), F32)
        for p2 in range(p + 1):
            same = across[p] == down[p2]
            if p2 == p:
                same = same & earlier
            rank = rank + jnp.sum(jnp.where(same, 1.0, 0.0), axis=0, keepdims=True)
        ranks.append(rank)
    to_plane = (slab // 8) * 4 + piece // 2
    to_column = (piece % 2) * 8 + slab % 8
    base = (to_plane * 64 + to_column * 4).astype(F32)
    position = [base[p:p + 1, :] + ranks[p] for p in range(4)]
    key4 = ((slot % 64) * 4 + iota((4, 128), 0) + 1).astype(F32)
    keys = jnp.concatenate([key4[p:p + 1, :] for p in range(4)], axis=1)
    keys16 = jnp.broadcast_to(keys, (16, 512)).astype(BF16)
    mine16 = iota((16, 128), 0) == u
    ins = rows_ins[...].astype(BF16)
    slot_iota = iota((128, 128), 0).astype(F32)

    def dispatch(chunk, _):
        where = slot_iota + (chunk * 128).astype(F32)
        pick = jnp.concatenate([jnp.where(where == position[p], 1.0, 0.0) for p in range(4)], axis=1).astype(BF16)
        data = dot(pick, ins).astype(BF16)
        meta = jnp.where(mine16, dot_nt(keys16, pick), 0.0).astype(BF16)
        for t in range(2):
            hop1_out[chunk * 2 + t, 0:64, :] = data[t * 64:(t + 1) * 64]
            hop1_out[chunk * 2 + t, 64:80, :] = meta
        return 0

    lax.fori_loop(0, 8, dispatch, 0, unroll=2)

    def h1_copy(i):
        to = plane(i)
        return copy(hop1_out.at[(u + i) % 16], hop1_in.at[u], h1_send.at[i], h1_recv.at[i], to[0], to[1])

    lax.fori_loop(1, 16, lambda i, _: (h1_copy(i).start(), 0)[1], 0)
    hop1_in[u] = hop1_out[u]

    def pass_proj(half):
        came_left(2 * half).wait_recv()
        pass_right(2 * half).start()
        came_right(2 * half + 1).wait_recv()
        pass_left(2 * half + 1).start()

    def pass_weight(half):
        @pl.when(relays)
        def _():
            w_copy(relay_from, relay_from * 2 + core, half, a).wait_recv()
            w_copy(z, relay_from * 2 + core, half, relay_to * 2 + core).start()
            t_copy(relay_from * 2 + core, half).start()

        for i in range(1, 4):
            source = (z + i) % 4

            @pl.when(jnp.logical_not(relays & (source == relay_from)))
            def _():
                w_copy(source, source * 2 + core, half, a).wait_recv()
                t_copy(source * 2 + core, half).start()

    def norms(k, _):
        low_tiles, high_tiles = [], []
        for e in range(8):
            q = k * 8 + e
            q_hi = q + 32
            ky = (jnp.where(odd8, -64, 0) + jnp.where(half8, q, q_hi)).astype(F32)
            radius = (kx2 + ky * ky) * (1.0 / 16384.0)
            n_lo = jnp.where(odd8, noise_full[pl.ds(q + 64, 1), :], noise_full[pl.ds(q, 1), :])
            n_hi = jnp.where(odd8, noise_full[pl.ds(q_hi + 64, 1), :], noise_full[pl.ds(q_hi, 1), :])
            outs_lo, outs_hi = [], []
            for b in range(8):
                squared = sine_squared(focus_in[b] * radius + 0.1)
                turned = pltpu.roll(squared, 64, 1)
                outs_lo.append(jnp.where(half8, squared, turned) * n_lo)
                outs_hi.append(jnp.where(half8, turned, squared) * n_hi)
            lanes = pl.ds(e * 128, 128)
            left_op[k, 192:256, lanes] = jnp.concatenate(outs_lo, axis=0).astype(BF16)
            left_op[k + 4, 192:256, lanes] = jnp.concatenate(outs_hi, axis=0).astype(BF16)
        return 0

    lane16 = iota((16, 128), 1)
    angle_x = (lane16 % 64).astype(F32) * (2.0 * PI / 128.0)
    cos_x = sine(angle_x + 0.5 * PI)
    sin_x = sine(angle_x) * jnp.where(lane16 < 64, 1.0, -1.0)
    angle_y = iota((64, 128), 0).astype(F32) * (2.0 * PI / 128.0)
    turn_tab[0] = sine(angle_y + 0.5 * PI)
    turn_tab[1] = sine(angle_y) * jnp.where(iota((64, 128), 1) < 64, -1.0, 1.0)
    flip16 = jnp.where(iota((16, 128), 0) % 2 == 1, -1.0, 1.0)

    def views(block, half):
        row = pl.multiple_of(block * 16, 16)

        def step(k, _):
            for e in range(8):
                q = k * 8 + e
                image_half = proj_in[block, pl.ds(pl.multiple_of(q * 16, 16), 16), :]
                image = image_half.astype(F32)
                lanes = pl.ds(e * 128, 128)
                w = image * (flip16 * turn_tab[0, pl.ds(q, 1), :])
                s = pltpu.roll(image, 64, 1) * (flip16 * turn_tab[1, pl.ds(q, 1), :])
                right_op[k, pl.ds(row, 16), lanes] = (w - s).astype(BF16)
                right_op[k, pl.ds(row + 64, 16), lanes] = image_half
                right_op[k, pl.ds(row + 128, 16), lanes] = (w + s).astype(BF16)
                right_op[k, pl.ds(row + 192, 16), lanes] = (image * image).astype(BF16)
            return 0

        lax.fori_loop(half * 4, half * 4 + 4, step, 0)

    def turns(zz, half):
        row = pl.multiple_of(zz * 16, 16)

        def step(k, _):
            for e2 in range(4):
                at = pl.ds(pl.multiple_of(k * 64 + e2 * 16, 16), 16)
                first = weight_in[zz * 2, at, :].astype(F32)
                second = weight_in[zz * 2 + 1, at, :].astype(F32)
                for e in range(2):
                    lanes = pl.ds((e2 * 2 + e) * 128, 128)
                    image = jnp.concatenate([first[e * 8:e * 8 + 8], second[e * 8:e * 8 + 8]], axis=0)
                    w = image * cos_x
                    s = pltpu.roll(image, 64, 1) * sin_x
                    left_op[k, pl.ds(row, 16), lanes] = (w - s).astype(BF16)
                    left_op[k, pl.ds(row + 64, 16), lanes] = image.astype(BF16)
                    left_op[k, pl.ds(row + 128, 16), lanes] = (w + s).astype(BF16)
            return 0

        lax.fori_loop(half * 4, half * 4 + 4, step, 0)

    def multiply(half):
        part = dot_nt(left_op[half * 4], right_op[half * 4])
        for k in range(1, 4):
            part = part + dot_nt(left_op[half * 4 + k], right_op[half * 4 + k])
        for h in range(2):
            lanes = part[:, h * 128:(h + 1) * 128]
            score[h] = lanes if half == 0 else score[h] + lanes

    pass_proj(0)
    lax.fori_loop(1, 8, lambda i, _: (f_copy(i).wait_recv(), 0)[1], 0)
    lax.fori_loop(0, 2, norms, 0)
    pass_weight(0)
    views(x, 0)
    lax.fori_loop(2, 4, norms, 0)
    pass_proj(1)
    views(x, 1)
    t_copy(a, 0).wait_recv()
    turns(z, 0)
    pass_weight(1)

    lax.fori_loop(1, 16, lambda i, _: (h1_copy(i).wait_recv(), 0)[1], 0)
    m_row, m_col = iota((256, 256), 0), iota((256, 256), 1)
    mix = jnp.where(m_col == ((m_row // 4) % 4) * 64 + (m_row // 16) * 4 + m_row % 4, 1.0, 0.0).astype(BF16)

    def regroup(group, _):
        four = jnp.concatenate([hop1_in[group * 4 + t, 0:64, :] for t in range(4)], axis=0)
        mixed = dot(mix, four).astype(BF16)
        at = pl.ds(pl.multiple_of(group * 16, 16), 16)
        for b in range(16):
            hop2_out[b, at, :] = mixed[b * 16:(b + 1) * 16]
        return 0

    lax.fori_loop(0, 4, regroup, 0)
    meta = hop1_in[0, 64:80, :].astype(F32)
    for t in range(1, 16):
        meta = meta + hop1_in[t, 64:80, :].astype(F32)
    meta = meta.astype(BF16)
    for b in range(16):
        hop2_out[b, 64:80, :] = meta

    def h2_copy(i):
        to = column(i)
        return copy(hop2_out.at[(v + i) % 16], hop2_in.at[v], h2_send.at[i], h2_recv.at[i], to[0], to[1])

    lax.fori_loop(1, 16, lambda i, _: (h2_copy(i).start(), 0)[1], 0)
    hop2_in[v] = hop2_out[v]

    came_left(1).wait_recv()
    came_right(0).wait_recv()
    views(from_left, 0)
    views(from_right, 0)
    for i in range(1, 4):
        source = (z + i) % 4
        t_copy(source * 2 + 1 - core, 0).wait_recv()
        turns(source, 0)
    came_across(0).wait_recv()
    came_across(1).wait_recv()
    views(across_x, 0)
    multiply(0)
    t_copy(a, 1).wait_recv()
    turns(z, 1)
    came_left(3).wait_recv()
    came_right(2).wait_recv()
    views(from_left, 1)
    views(from_right, 1)
    came_across(2).wait_recv()
    came_across(3).wait_recv()
    views(across_x, 1)
    for i in range(1, 4):
        source = (z + i) % 4
        t_copy(source * 2 + 1 - core, 1).wait_recv()
        turns(source, 1)
    multiply(1)

    even = jnp.concatenate([score[h, pl.ds(0, 128, stride=2), :] for h in range(2)], axis=1)
    odd = jnp.concatenate([score[h, pl.ds(1, 128, stride=2), :] for h in range(2)], axis=1)
    folded = even + pltpu.roll(odd, 255, 1)
    lane32 = iota((32, 128), 1)
    penalty = folded[96:128, 128:256]
    penalty = 0.5 * jnp.where(lane32 < 64, pltpu.roll(penalty, 64, 1), penalty)
    penalty = jnp.concatenate([penalty, penalty], axis=1)
    lane = iota((32, 256), 1)
    valid = (lane % 2 == 0) & (lane < 192)
    scores = [jnp.where(valid, folded[s * 32:(s + 1) * 32, :] - penalty, -3e38) for s in range(3)]
    top_score = jnp.max(jnp.maximum(jnp.maximum(scores[0], scores[1]), scores[2]), axis=1, keepdims=True)
    weight = sum(jnp.where(valid, jnp.exp(s - top_score), 0.0) for s in scores)
    same_class = jnp.where((m_row // 2) % 8 == m_col % 8, 1.0, 0.0).astype(BF16)
    own = lane // 8 == iota((32, 256), 0)
    sums = jnp.sum(jnp.where(own, split_dot(weight, same_class), 0.0), axis=0, keepdims=True)
    tops = jnp.sum(jnp.where(own, top_score, 0.0), axis=0, keepdims=True)
    tile = jnp.where(row8 == 0, sums[:, 0:128], 0.0)
    tile = jnp.where(row8 == 1, sums[:, 128:256], tile)
    tile = jnp.where(row8 == 2, tops[:, 0:128], tile)
    stat[a] = jnp.where(row8 == 3, tops[:, 128:256], tile)

    def s_copy(i):
        to = alpha(i)
        return copy(stat.at[a], stat.at[a], s_send.at[i], s_recv.at[i], to[0], to[1])

    for i in range(1, 8):
        s_copy(i).start()

    for part in range(4):
        to_right(part).wait_send()
        to_left(part).wait_send()
    for half in range(2):
        pass_right(2 * half).wait_send()
        pass_left(2 * half + 1).wait_send()
        each_z(lambda target: w_copy(target, a, half, target * 2 + core).wait_send())

        @pl.when(relays)
        def _():
            w_copy(z, relay_from * 2 + core, half, relay_to * 2 + core).wait_send()

        for zz in range(4):
            t_copy(zz * 2 + core, half).wait_send()
    lax.fori_loop(1, 8, lambda i, _: (f_copy(i).wait_send(), 0)[1], 0)
    lax.fori_loop(1, 16, lambda i, _: (h1_copy(i).wait_send(), 0)[1], 0)

    for i in range(1, 8):
        s_copy(i).wait_recv()
    best = stat[0]
    for b in range(1, 8):
        best = jnp.maximum(best, stat[b])
    total = jnp.zeros((8, 128), F32)
    for b in range(8):
        tile = stat[b]
        total = total + tile * pltpu.roll(jnp.exp(tile - best), 6, 0)
    total = jnp.where(row8 < 2, total, 0.0)
    o_row, o_col = iota((128, 128), 0), iota((128, 128), 1)
    same_particle = jnp.where(o_row // 8 == o_col // 8, 1.0, 0.0).astype(BF16)
    class_w = jnp.where(row8 < 2, total / split_dot(total, same_particle), 0.0)
    first, second = class_w[0:1, :], class_w[1:2, :]
    tile = jnp.where(row8 == (u % 4) * 2, first, 0.0)
    cwt[g] = jnp.where(row8 == (u % 4) * 2 + 1, second, tile)

    def c_copy(i):
        to = gamma(i)
        return copy(cwt.at[g], cwt.at[g], c_send.at[i], c_recv.at[i], to[0], to[1])

    for i in range(1, 32):
        c_copy(i).start()

    flat = jnp.concatenate([first, second], axis=1)
    spread = jnp.where(iota((8, 256), 1) // 8 == iota((8, 256), 0) + a * 4, flat, 0.0)
    gather_class = jnp.where(iota((256, 128), 0) % 8 == iota((256, 128), 1), 1.0, 0.0).astype(BF16)
    hi = spread.astype(BF16)
    rest = spread - hi.astype(F32)
    cw_flat[...] = dot(hi, gather_class) + split_dot(rest, gather_class)
    cw_ref[...] = cw_flat[0:4, 0:8]

    for i in range(1, 8):
        s_copy(i).wait_send()
    lax.fori_loop(1, 16, lambda i, _: (h2_copy(i).wait_send(), 0)[1], 0)
    lax.fori_loop(1, 16, lambda i, _: (h2_copy(i).wait_recv(), 0)[1], 0)
    pick_key = jnp.where(o_row == (u % 2) * 64 + v * 4 + o_col % 4, 1.0, 0.0).astype(BF16)
    own_source = lane32 // 4 == iota((32, 128), 0)
    slot64 = iota((64, 128), 0).astype(F32)
    repeats = [
        jnp.where(o_row == (t // 2) * 32 + ((o_col % 64) // 4) * 2 + t % 2, 1.0, 0.0).astype(BF16) for t in range(4)
    ]
    lax.fori_loop(1, 32, lambda i, _: (c_copy(i).wait_recv(), 0)[1], 0)

    gathered = []
    for group in range(8):
        tile = cwt[group * 4]
        for t in range(1, 4):
            tile = tile + cwt[group * 4 + t]
        gathered.append(tile)
    table = jnp.concatenate(gathered + [jnp.zeros((64, 128), F32)], axis=0).T.astype(BF16)
    for t in range(4):
        coef_tab[t] = dot(table, repeats[t])
    vol_ref[...] = jnp.zeros_like(vol_ref)

    def insert(quad, _):
        parts, rows_in = [], []
        for h in range(2):
            w = quad * 2 + h
            tags = jnp.concatenate([hop2_in[w * 2, 64:80, :], hop2_in[w * 2 + 1, 64:80, :]], axis=0)
            key = jnp.sum(jnp.where(own_source, dot(tags, pick_key), 0.0), axis=0, keepdims=True) - 1.0
            at_slot = jnp.floor(key * 0.25)
            which = key - 4.0 * at_slot
            coef = jnp.zeros((8, 128), F32)
            for p in range(4):
                even_core = coef_tab[quad, h * 64 + p * 8:h * 64 + p * 8 + 8, :]
                odd_core = coef_tab[quad, h * 64 + 32 + p * 8:h * 64 + 40 + p * 8, :]
                coef = jnp.where(which == float(p), jnp.where(half8, even_core, odd_core), coef)
            hit = slot64 == at_slot
            parts.append(
                jnp.concatenate([jnp.where(hit, coef[c:c + 1, :], 0.0) for c in range(8)], axis=0).astype(BF16)
            )
            rows_in += [hop2_in[w * 2, 0:64, :], hop2_in[w * 2 + 1, 0:64, :]]
        vol_ref[...] += dot(jnp.concatenate(parts, axis=1), jnp.concatenate(rows_in, axis=0))
        return 0

    lax.fori_loop(0, 4, insert, 0)
    lax.fori_loop(1, 32, lambda i, _: (c_copy(i).wait_send(), 0)[1], 0)


def per_device(particles, defocus, noise_weight, projections, row_slab, row_slot, interp):
    vmem, dma = pltpu.VMEM, pltpu.SemaphoreType.DMA
    volume, class_weight = pl.pallas_call(
        kernel,
        out_shape=(jax.ShapeDtypeStruct((512, 128), F32), jax.ShapeDtypeStruct((4, 8), F32)),
        in_specs=[pl.BlockSpec(memory_space=pl.ANY)] * 7,
        out_specs=(pl.BlockSpec(memory_space=vmem), pl.BlockSpec(memory_space=vmem)),
        scratch_shapes=[
            vmem((512, 128), BF16),
            vmem((1, 4), F32),
            vmem((64, 128), F32),
            vmem((1024, 128), BF16),
            vmem((4, 128), jnp.int32),
            vmem((4, 128), jnp.int32),
            vmem((4, 128), F32),
            vmem((512, 128), F32),
            vmem((1024, 128), F32),
            vmem((128, 128), F32),
            vmem((512, 128), F32),
            vmem((8, 512, 128), BF16),
            vmem((4, 1024, 128), BF16),
            vmem((8, 8, 128), F32),
            vmem((512, 128), F32),
            vmem((8, 256, 1024), BF16),
            vmem((8, 256, 1024), BF16),
            vmem((2, 256, 128), F32),
            vmem((2, 64, 128), F32),
            vmem((16, 80, 128), BF16),
            vmem((16, 80, 128), BF16),
            vmem((16, 80, 128), BF16),
            vmem((16, 80, 128), BF16),
            vmem((8, 8, 128), F32),
            vmem((32, 8, 128), F32),
            vmem((8, 128), F32),
            vmem((4, 128, 128), F32),
            dma((7,)), dma((8,)), dma((8,)), dma((8,)), dma((8,)), dma((12,)), dma((12,)), dma((8,)), dma((8,)),
            dma((16,)), dma((16,)), dma((16,)), dma((16,)), dma((8,)), dma((8,)), dma((32,)), dma((32,)),
        ],
        compiler_params=pltpu.CompilerParams(
            collective_id=0, has_side_effects=True, vmem_limit_bytes=56 * 1024 * 1024
        ),
    )(
        particles.reshape(512, 128), defocus.reshape(1, 4), noise_weight.T, projections.reshape(1024, 128),
        row_slab.reshape(4, 128), row_slot, interp,
    )
    return volume.reshape(8, 64, 128), class_weight


def solution(mesh):
    in_specs = (
        P(("blk", "dom"), None, None),
        P(("blk", "dom")),
        P(),
        P(None, "blk", None, None),
        P(("blk", "dom"), None, None),
        P(("blk", "dom"), None),
        P(("blk", "dom"), None),
    )
    out_specs = (P(None, ("blk", "dom"), None), P(("blk", "dom"), None))
    return jax.shard_map(per_device, mesh=mesh, in_specs=in_specs, out_specs=out_specs, check_vma=False)
```

time: 67.4 us -> 52.6 us (0.78)
  Pallas kernels: 61.5 us -> 49.6 us
  local copies, waits for them, and re-layouts: 4.91 us -> 2.25 us
    pallas_call x1, Pallas kernels: 61.5 us -> 49.6 us  [per_device(): pl.pallas_call(kernel, out_shape=(jax.ShapeDtypeStruct((512, 128), F32),...]
    unnamed x15 -> x4, local copies, waits for them, and re-layouts: 4.68 us -> 2.25 us
where the time goes in v1:
time: 52.6 us; the launch traced here: 52.5 us
  Pallas kernels  49.6 us (94%)
  local copies, waits for them, and re-layouts  2.25 us (4%)
  between operations  0.65 us (1%)
    pallas_call x1, Pallas kernels, per_device(): pl.pallas_call(kernel, out_shape=(jax.ShapeDtypeStruct((512, 128), F32),...  49.6 us
    unnamed x4, local copies, waits for them, and re-layouts  2.25 us

profile of v1, /device:TPU:1, one launch (start us, length us, event | category | flops | bytes accessed | tf_op | source)
XLA Modules:
  0.0 52.5 jit_solution(2608240453457599096)
XLA Ops:
  0.6 49.6 %shard_map.86 = (f32[512,128]{1,0:T(8,128)}, f32[4,8]{1,0:T(4,128)}) custom-call(bf16[512,128]{1,0:T(8,128)(2,1)} %bitcast.8, f32[1,4]{1,0:T(1,128)} %bitcast.11, f32[64,128]{1,0:T(8,128)} %bitcast.9, bf16[1024,128]{1,0:T(8,128)(2,1)} %bitcast.6, s32[4,128]{1,0:T(4,128)} %bitcast.10, s32[4,128]{1,0:T(4,128)} %slot_hbm.1, f32[4,128]{1,0:T(4,128)} %interp_hbm.1), custom_call_target="tpu_custom_call" | custom-call | tf_op jit(solution)/shard_map/pallas_call | solution.py:581
  50.2 0.0 copy-start
  50.2 1.7 %copy.11 = f32[8,64,128]{2,1,0:T(8,128)} copy(f32[8,64,128]{2,1,0:T(8,128)} %bitcast.7) | data formatting | bytes 524288
  51.9 0.0 copy-done
  51.9 0.6 %copy.12 = f32[4,8]{1,0:T(4,128)} copy(f32[4,8]{1,0:T(4,128)S(1)} %copy-done) | data formatting | bytes 256
Async XLA Ops:
  50.2 1.7 %copy-start = (f32[4,8]{1,0:T(4,128)S(1)}, f32[4,8]{1,0:T(4,128)}, u32[]{:S(2)}) copy-start(f32[4,8]{1,0:T(4,128)} %get-tuple-element.9) | copy-start | bytes 388

commit v2 on v1

v2 whole, which is shorter than its diff:
```python
import jax
import jax.numpy as jnp
from jax import lax
from jax.experimental import pallas as pl
from jax.experimental.pallas import tpu as pltpu
from jax.sharding import PartitionSpec as P

F32, BF16 = jnp.float32, jnp.bfloat16
MESH = pl.DeviceIdType.MESH
PI = 3.141592653589793
SIN_COEF = (
    0.9999999992267364, -0.16666665898756483, 0.008333320916259667, -0.00019840515744570079,
    2.7535452887970435e-06, -2.47248903062851e-08, 1.3598699876951359e-10,
)
SIN2_COEF = (
    0.9999999902438815, -0.3333330511544617, 0.044443119935340766, -0.00317232337316227,
    0.00013931019440764148, -3.6240280738953943e-06,
)


def reduced(angle, period, high, mid):
    turns = jnp.floor(angle * (1.0 / period) + 0.5)
    return ((angle - turns * high) - turns * mid) - turns * (period - high - mid)


def horner(coef, y):
    total = jnp.full_like(y, coef[-1])
    for c in coef[-2::-1]:
        total = total * y + c
    return total


def sine(angle):
    r = reduced(angle, 2 * PI, 6.28125, 8117 / 2**22)
    return r * horner(SIN_COEF, r * r)


def sine_squared(angle):
    r = reduced(angle, PI, 3.140625, 8117 / 2**23)
    y = r * r
    return y * horner(SIN2_COEF, y)


def iota(shape, axis):
    return lax.broadcasted_iota(jnp.int32, shape, axis)


def dot(a, b):
    return jnp.dot(a, b, preferred_element_type=F32)


def dot_nt(a, b):
    return lax.dot_general(a, b, (((1,), (1,)), ((), ())), preferred_element_type=F32)


def split_dot(values, indicator):
    high = values.astype(BF16)
    low = (values - high.astype(F32)).astype(BF16)
    return dot(high, indicator) + dot(low, indicator)


def kernel(
    part_hbm, focus_hbm, noise_hbm, proj_hbm, slab_hbm, slot_hbm, interp_hbm,
    vol_ref, cw_ref,
    part_ref, focus_ref, noise_ref, proj_ref, slab_ref, slot_ref, interp_ref,
    wide_p, wide_x, noise_full, cols, weight_in, proj_in, rows_ins,
    left_op, right_op, score, turn_tab, hop1_out, hop1_in, hop2_out, hop2_in,
    stat, cw_in, cw_flat, coef_tab,
    in_sem, w_send, w_recv, t_send, t_recv, p_send, p_recv, h1_send, h1_recv, h2_send, h2_recv,
    s_send, s_recv, c_send, c_recv,
):
    blk, dom = lax.axis_index("blk"), lax.axis_index("dom")
    x, a = blk // 8, blk % 8
    z, core = a // 2, a % 2
    y, z_hi = dom // 2, dom % 2
    u = x * 4 + y
    z_full = z_hi * 4 + z
    v = z_full * 2 + core

    def copy(src, dst, send, recv, to_blk, to_dom):
        return pltpu.make_async_remote_copy(
            src_ref=src, dst_ref=dst, send_sem=send, recv_sem=recv,
            device_id=(to_blk, to_dom), device_id_type=MESH,
        )

    def fetch(k, src, dst):
        return pltpu.make_async_copy(src, dst, in_sem.at[k])

    fetches = [
        fetch(0, part_hbm, part_ref), fetch(1, focus_hbm, focus_ref), fetch(2, noise_hbm, noise_ref),
        fetch(3, interp_hbm, interp_ref), fetch(4, proj_hbm, proj_ref), fetch(5, slab_hbm, slab_ref),
        fetch(6, slot_hbm, slot_ref),
    ]
    for f in fetches:
        f.start()

    other = x * 8 + z * 2 + 1 - core

    def plane(i):
        to = (u + i) % 16
        return (to // 4) * 8 + a, (to % 4) * 2 + z_hi

    def column(i):
        to = (v + i) % 16
        return x * 8 + to % 8, y * 2 + to // 8

    barrier = pltpu.get_barrier_semaphore()

    def greet(who):
        def send(i, _):
            pl.semaphore_signal(barrier, inc=1, device_id=who(i), device_id_type=MESH)
            return 0

        return send

    right, left = ((x + 1) % 4) * 8 + a, ((x + 3) % 4) * 8 + a
    from_left, from_right, across_x = (x + 3) % 4, (x + 1) % 4, (x + 2) % 4
    lax.fori_loop(1, 16, greet(column), 0)
    lax.fori_loop(1, 16, greet(plane), 0)

    def p_copy(k, block, part, to):
        rows = pl.ds(part * 512, 512)
        return copy(proj_in.at[block, rows], proj_in.at[block, rows], p_send.at[k], p_recv.at[k], to, dom)

    def to_right(part):
        return p_copy(part, x, part, right)

    def to_left(part):
        return p_copy(2 + part, x, part, left)

    def came_left(part):
        return p_copy(part, from_left, part, right)

    def came_right(part):
        return p_copy(2 + part, from_right, part, left)

    def pass_right():
        return p_copy(4, from_left, 0, right)

    def pass_left():
        return p_copy(5, from_right, 1, left)

    def w_copy(k, block, to):
        return copy(
            weight_in.at[block], weight_in.at[block], w_send.at[k], w_recv.at[block // 2], x * 8 + to, dom
        )

    def t_copy(block):
        return copy(
            weight_in.at[block], weight_in.at[block], t_send.at[block // 2], t_recv.at[block // 2], other, dom
        )

    def each_z(act):
        for away in (2, 1):
            for sign in (1, -1):
                target = z + sign * away

                @pl.when((target >= 0) & (target < 4))
                def _():
                    act(target)

    relays = (z == 1) | (z == 2)
    relay_from, relay_to = (2 - z) * 3, (z - 1) * 3

    lane8 = iota((8, 128), 1)
    row8 = iota((8, 128), 0)
    kx = (lane8 % 64).astype(F32)
    kx2 = kx * kx
    odd8 = (row8 % 2) == 1
    half8 = lane8 < 64

    for k in (1, 2, 3):
        fetches[k].wait()
    noise_half = noise_ref[...]
    noise_full[...] = jnp.concatenate([noise_half, noise_half], axis=0).T
    interp = interp_ref[...]
    for p in range(4):
        cols[p * 128:(p + 1) * 128, :] = jnp.broadcast_to(interp[p:p + 1, :], (128, 128)).T
    lane4 = iota((8, 4), 1)
    focus4 = jnp.broadcast_to(focus_ref[...], (8, 4))
    focus = jnp.sum(jnp.where(lane4 == iota((8, 4), 0) // 2, focus4, 0.0), axis=1, keepdims=True)
    focus = jnp.broadcast_to(focus, (8, 128))
    focus_hi = focus.astype(BF16).astype(F32)
    focus_mid = (focus - focus_hi).astype(BF16).astype(F32)
    weight_in[a, 512:544, :] = jnp.concatenate(
        [focus_hi, focus_mid, focus - focus_hi - focus_mid, jnp.zeros_like(focus)], axis=0
    ).astype(BF16)
    fetches[0].wait()
    wide_p[...] = part_ref[...].astype(F32)

    def weigh(q2, _):
        tiles = []
        for h in range(2):
            q = q2 * 2 + h
            rows = pl.ds(q, 8, stride=64)
            image = wide_p[rows, :]
            ky = jnp.where(odd8, q - 64, q).astype(F32)
            radius = (kx2 + ky * ky) * (1.0 / 16384.0)
            signal = -sine(focus * radius + 0.1) * image
            noise = jnp.where(odd8, noise_full[pl.ds(q + 64, 1), :], noise_full[pl.ds(q, 1), :])
            tiles.append(signal * noise)
            rows_ins[rows, :] = signal * cols[rows, :]
        weight_in[a, pl.ds(pl.multiple_of(q2 * 16, 16), 16), :] = jnp.concatenate(tiles, axis=0).astype(BF16)
        return 0

    def order_proj(q, _):
        tile = wide_x[pl.ds(q, 16, stride=64), :].astype(BF16)
        proj_in[x, pl.ds(pl.multiple_of(q * 16, 16), 16), :] = tile
        return 0

    lax.fori_loop(0, 32, weigh, 0, unroll=4)
    fetches[4].wait()
    wide_x[...] = proj_ref[...].astype(F32)
    lax.fori_loop(0, 64, order_proj, 0, unroll=8)

    fetches[5].wait()
    fetches[6].wait()
    slab, slot = slab_ref[...], slot_ref[...]
    piece = slot // 64
    bucket = (slab * 8 + piece).astype(F32)
    earlier = iota((128, 128), 0) < iota((128, 128), 1)
    ranks = []
    across = [jnp.broadcast_to(bucket[p:p + 1, :], (128, 128)) for p in range(4)]
    down = [b.T for b in across]
    for p in range(4):
        rank = jnp.zeros((1, 128), F32)
        for p2 in range(p + 1):
            same = across[p] == down[p2]
            if p2 == p:
                same = same & earlier
            rank = rank + jnp.sum(jnp.where(same, 1.0, 0.0), axis=0, keepdims=True)
        ranks.append(rank)
    to_plane = (slab // 8) * 4 + piece // 2
    to_column = (piece % 2) * 8 + slab % 8
    base = (to_plane * 64 + to_column * 4).astype(F32)
    position = [base[p:p + 1, :] + ranks[p] for p in range(4)]
    key4 = ((slot % 64) * 4 + iota((4, 128), 0) + 1).astype(F32)
    keys = jnp.concatenate([key4[p:p + 1, :] for p in range(4)], axis=1)
    keys16 = jnp.broadcast_to(keys, (16, 512)).astype(BF16)
    mine16 = iota((16, 128), 0) == u
    ins = rows_ins[...].astype(BF16)
    slot_iota = iota((128, 128), 0).astype(F32)

    def dispatch(chunk, _):
        where = slot_iota + (chunk * 128).astype(F32)
        pick = jnp.concatenate([jnp.where(where == position[p], 1.0, 0.0) for p in range(4)], axis=1).astype(BF16)
        data = dot(pick, ins).astype(BF16)
        tags = dot_nt(keys16, pick)
        for t in range(2):
            meta = tags if t == 0 else pltpu.roll(tags, 64, 1)
            hop1_out[chunk * 2 + t, 0:64, :] = data[t * 64:(t + 1) * 64]
            hop1_out[chunk * 2 + t, 64:80, :] = jnp.where(mine16, meta, 0.0).astype(BF16)
        return 0

    lax.fori_loop(0, 8, dispatch, 0, unroll=2)

    pl.semaphore_wait(barrier, 30)
    each_z(lambda target: w_copy(target, a, target * 2 + core).start())
    t_copy(a).start()
    to_right(0).start()
    to_left(1).start()
    to_right(1).start()
    to_left(0).start()

    def h1_copy(i):
        to = plane(i)
        return copy(hop1_out.at[(u + i) % 16], hop1_in.at[u], h1_send.at[i], h1_recv.at[i], to[0], to[1])

    lax.fori_loop(1, 16, lambda i, _: (h1_copy(i).start(), 0)[1], 0)
    hop1_in[u] = hop1_out[u]

    lane16 = iota((16, 128), 1)
    angle_x = (lane16 % 64).astype(F32) * (2.0 * PI / 128.0)
    cos_x = sine(angle_x + 0.5 * PI)
    sin_x = sine(angle_x) * jnp.where(lane16 < 64, 1.0, -1.0)
    angle_y = iota((64, 128), 0).astype(F32) * (2.0 * PI / 128.0)
    turn_tab[0] = sine(angle_y + 0.5 * PI)
    turn_tab[1] = sine(angle_y) * jnp.where(iota((64, 128), 1) < 64, -1.0, 1.0)
    flip16 = jnp.where(iota((16, 128), 0) % 2 == 1, -1.0, 1.0)

    def views(block):
        row = pl.multiple_of(block * 16, 16)

        def step(k, _):
            for e in range(8):
                q = k * 8 + e
                image_half = proj_in[block, pl.ds(pl.multiple_of(q * 16, 16), 16), :]
                image = image_half.astype(F32)
                lanes = pl.ds(e * 128, 128)
                w = image * (flip16 * turn_tab[0, pl.ds(q, 1), :])
                s = pltpu.roll(image, 64, 1) * (flip16 * turn_tab[1, pl.ds(q, 1), :])
                right_op[k, pl.ds(row, 16), lanes] = (w - s).astype(BF16)
                right_op[k, pl.ds(row + 64, 16), lanes] = image_half
                right_op[k, pl.ds(row + 128, 16), lanes] = (w + s).astype(BF16)
                right_op[k, pl.ds(row + 192, 16), lanes] = (image * image).astype(BF16)
            return 0

        lax.fori_loop(0, 8, step, 0)

    def turns(zz):
        row = pl.multiple_of(zz * 16, 16)
        focus_of = []
        for b in range(2):
            parts = weight_in[zz * 2 + b, 512:544, :].astype(F32)
            focus_of.append(parts[0:8] + parts[8:16] + parts[16:24])

        def step(k, _):
            for e2 in range(4):
                at = pl.ds(pl.multiple_of(k * 64 + e2 * 16, 16), 16)
                first = weight_in[zz * 2, at, :].astype(F32)
                second = weight_in[zz * 2 + 1, at, :].astype(F32)
                for e in range(2):
                    lanes = pl.ds((e2 * 2 + e) * 128, 128)
                    image = jnp.concatenate([first[e * 8:e * 8 + 8], second[e * 8:e * 8 + 8]], axis=0)
                    w = image * cos_x
                    s = pltpu.roll(image, 64, 1) * sin_x
                    left_op[k, pl.ds(row, 16), lanes] = (w - s).astype(BF16)
                    left_op[k, pl.ds(row + 64, 16), lanes] = image.astype(BF16)
                    left_op[k, pl.ds(row + 128, 16), lanes] = (w + s).astype(BF16)
            return 0

        lax.fori_loop(0, 8, step, 0)

        def norms(k, _):
            for e in range(8):
                q = k * 8 + e
                q_hi = q + 32
                ky = (jnp.where(odd8, -64, 0) + jnp.where(half8, q, q_hi)).astype(F32)
                radius = (kx2 + ky * ky) * (1.0 / 16384.0)
                n_lo = jnp.where(odd8, noise_full[pl.ds(q + 64, 1), :], noise_full[pl.ds(q, 1), :])
                n_hi = jnp.where(odd8, noise_full[pl.ds(q_hi + 64, 1), :], noise_full[pl.ds(q_hi, 1), :])
                outs_lo, outs_hi = [], []
                for b in range(2):
                    squared = sine_squared(focus_of[b] * radius + 0.1)
                    turned = pltpu.roll(squared, 64, 1)
                    outs_lo.append(jnp.where(half8, squared, turned) * n_lo)
                    outs_hi.append(jnp.where(half8, turned, squared) * n_hi)
                lanes = pl.ds(e * 128, 128)
                left_op[k, pl.ds(row + 192, 16), lanes] = jnp.concatenate(outs_lo, axis=0).astype(BF16)
                left_op[k + 4, pl.ds(row + 192, 16), lanes] = jnp.concatenate(outs_hi, axis=0).astype(BF16)
            return 0

        lax.fori_loop(0, 4, norms, 0)

    views(x)

    t_copy(a).wait_recv()
    turns(z)
    came_left(0).wait_recv()
    pass_right().start()
    came_right(1).wait_recv()
    pass_left().start()

    @pl.when(relays)
    def _():
        w_copy(relay_from, relay_from * 2 + core, a).wait_recv()
        w_copy(z, relay_from * 2 + core, relay_to * 2 + core).start()
        t_copy(relay_from * 2 + core).start()

    by_distance = (z + 1 - 2 * (z % 2), 2 - z // 2, 3 - 3 * (z // 2))
    for source in by_distance:

        @pl.when(jnp.logical_not(relays & (source == relay_from)))
        def _():
            w_copy(source, source * 2 + core, a).wait_recv()
            t_copy(source * 2 + core).start()

    came_left(1).wait_recv()
    views(from_left)
    came_right(0).wait_recv()
    views(from_right)
    for source in by_distance:
        t_copy(source * 2 + 1 - core).wait_recv()
        turns(source)
    p_copy(4, across_x, 0, right).wait_recv()
    p_copy(5, across_x, 1, left).wait_recv()
    views(across_x)

    part = dot_nt(left_op[0], right_op[0])
    for k in range(1, 8):
        part = part + dot_nt(left_op[k], right_op[k])
    for h in range(2):
        score[h] = part[:, h * 128:(h + 1) * 128]

    m_row, m_col = iota((256, 256), 0), iota((256, 256), 1)
    even = jnp.concatenate([score[h, pl.ds(0, 128, stride=2), :] for h in range(2)], axis=1)
    odd = jnp.concatenate([score[h, pl.ds(1, 128, stride=2), :] for h in range(2)], axis=1)
    folded = even + pltpu.roll(odd, 255, 1)
    lane32 = iota((32, 128), 1)
    penalty = folded[96:128, 128:256]
    penalty = 0.5 * jnp.where(lane32 < 64, pltpu.roll(penalty, 64, 1), penalty)
    penalty = jnp.concatenate([penalty, penalty], axis=1)
    lane = iota((32, 256), 1)
    valid = (lane % 2 == 0) & (lane < 192)
    scores = [jnp.where(valid, folded[s * 32:(s + 1) * 32, :] - penalty, -3e38) for s in range(3)]
    top_score = jnp.max(jnp.maximum(jnp.maximum(scores[0], scores[1]), scores[2]), axis=1, keepdims=True)
    weight = sum(jnp.where(valid, jnp.exp(s - top_score), 0.0) for s in scores)
    same_class = jnp.where((m_row // 2) % 8 == m_col % 8, 1.0, 0.0).astype(BF16)
    own = lane // 8 == iota((32, 256), 0)
    sums = jnp.sum(jnp.where(own, split_dot(weight, same_class), 0.0), axis=0, keepdims=True)
    tops = jnp.sum(jnp.where(own, top_score, 0.0), axis=0, keepdims=True)
    tile = jnp.where(row8 == 0, sums[:, 0:128], 0.0)
    tile = jnp.where(row8 == 1, sums[:, 128:256], tile)
    tile = jnp.where(row8 == 2, tops[:, 0:128], tile)
    stat[v] = jnp.where(row8 == 3, tops[:, 128:256], tile)

    def combine(tiles):
        best = tiles[0]
        for tile in tiles[1:]:
            best = jnp.maximum(best, tile)
        total = jnp.zeros((8, 128), F32)
        for tile in tiles:
            total = total + tile * pltpu.roll(jnp.exp(tile - best), 6, 0)
        return total

    def s_copy(i):
        to = column(i)
        return copy(stat.at[v], stat.at[v], s_send.at[i], s_recv.at[i], to[0], to[1])

    for i in (8, 7, 9, 6, 10, 5, 11, 4, 12, 3, 13, 2, 14, 1, 15):
        s_copy(i).start()

    lax.fori_loop(1, 16, lambda i, _: (h1_copy(i).wait_recv(), 0)[1], 0)
    mix = jnp.where(m_col == ((m_row // 4) % 4) * 64 + (m_row // 16) * 4 + m_row % 4, 1.0, 0.0).astype(BF16)

    def regroup(group, _):
        four = jnp.concatenate([hop1_in[group * 4 + t, 0:64, :] for t in range(4)], axis=0)
        mixed = dot(mix, four).astype(BF16)
        at = pl.ds(pl.multiple_of(group * 16, 16), 16)
        for b in range(16):
            hop2_out[b, at, :] = mixed[b * 16:(b + 1) * 16]
        return 0

    lax.fori_loop(0, 4, regroup, 0)
    meta = hop1_in[0, 64:80, :].astype(F32)
    for t in range(1, 16):
        meta = meta + hop1_in[t, 64:80, :].astype(F32)
    meta = meta.astype(BF16)
    for b in range(16):
        hop2_out[b, 64:80, :] = meta

    def h2_copy(i):
        to = column(i)
        return copy(hop2_out.at[(v + i) % 16], hop2_in.at[v], h2_send.at[i], h2_recv.at[i], to[0], to[1])

    lax.fori_loop(1, 16, lambda i, _: (h2_copy(i).start(), 0)[1], 0)
    hop2_in[v] = hop2_out[v]
    for part in range(2):
        to_right(part).wait_send()
        to_left(part).wait_send()
    pass_right().wait_send()
    pass_left().wait_send()
    each_z(lambda target: w_copy(target, a, target * 2 + core).wait_send())

    @pl.when(relays)
    def _():
        w_copy(z, relay_from * 2 + core, relay_to * 2 + core).wait_send()

    for zz in range(4):
        t_copy(zz * 2 + core).wait_send()
    lax.fori_loop(1, 16, lambda i, _: (h1_copy(i).wait_send(), 0)[1], 0)

    for i in range(1, 16):
        s_copy(i).wait_recv()
    near = combine([stat[i] for i in range(8)])
    far = combine([stat[i] for i in range(8, 16)])
    total = jnp.where(row8 < 2, near, jnp.where(row8 < 4, pltpu.roll(far, 2, 0), 0.0))
    o_row, o_col = iota((128, 128), 0), iota((128, 128), 1)
    same_particle = jnp.where(o_row // 8 == o_col // 8, 1.0, 0.0).astype(BF16)
    class_w = jnp.where(row8 < 4, total / split_dot(total, same_particle), 0.0)
    cw_in[u] = jnp.where(u % 2 == 0, class_w, pltpu.roll(class_w, 4, 0))

    def c_copy(i):
        to = plane(i)
        return copy(cw_in.at[u], cw_in.at[u], c_send.at[i], c_recv.at[i], to[0], to[1])

    for i in (10, 6, 9, 11, 5, 7, 8, 2, 14, 1, 3, 4, 12, 13, 15):
        c_copy(i).start()

    flat = jnp.sum(jnp.where(row8 == z_hi * 2 + z // 2, class_w, 0.0), axis=0, keepdims=True)
    spread = jnp.where(lane8 // 8 == row8 + (z % 2) * 8 + core * 4, flat, 0.0)
    gather_class = jnp.where(o_row % 8 == o_col, 1.0, 0.0).astype(BF16)
    hi = spread.astype(BF16)
    rest = spread - hi.astype(F32)
    cw_flat[...] = dot(hi, gather_class) + split_dot(rest, gather_class)
    cw_ref[...] = cw_flat[0:4, 0:8]

    for i in range(1, 16):
        s_copy(i).wait_send()
    lax.fori_loop(1, 16, lambda i, _: (h2_copy(i).wait_send(), 0)[1], 0)
    lax.fori_loop(1, 16, lambda i, _: (h2_copy(i).wait_recv(), 0)[1], 0)
    pick_key = jnp.where(o_row == v * 4 + o_col % 4, 1.0, 0.0).astype(BF16)
    own_source = lane32 // 4 == iota((32, 128), 0)
    slot64 = iota((64, 128), 0).astype(F32)
    repeats = [jnp.where(o_row == ((o_col % 64) // 4) * 4 + t, 1.0, 0.0).astype(BF16) for t in range(4)]
    vol_ref[...] = jnp.zeros_like(vol_ref)
    lax.fori_loop(1, 16, lambda i, _: (c_copy(i).wait_recv(), 0)[1], 0)

    gathered = [cw_in[2 * m] + cw_in[2 * m + 1] for m in range(8)]
    table = jnp.concatenate(gathered + [jnp.zeros((64, 128), F32)], axis=0).T.astype(BF16)
    for t in range(4):
        coef_tab[t] = dot(table, repeats[t])

    def insert(quad, _):
        parts, rows_in = [], []
        for h in range(2):
            w = quad * 2 + h
            tags = jnp.concatenate([hop2_in[w * 2, 64:80, :], hop2_in[w * 2 + 1, 64:80, :]], axis=0)
            key = jnp.sum(jnp.where(own_source, dot(tags, pick_key), 0.0), axis=0, keepdims=True) - 1.0
            at_slot = jnp.floor(key * 0.25)
            which = key - 4.0 * at_slot
            coef = jnp.zeros((8, 128), F32)
            for p in range(4):
                rows = h * 64 + p * 8
                both = jnp.where(half8, coef_tab[quad, rows:rows + 8, :], coef_tab[quad, rows + 32:rows + 40, :])
                coef = jnp.where(which == float(p), both, coef)
            hit = slot64 == at_slot
            parts.append(
                jnp.concatenate([jnp.where(hit, coef[c:c + 1, :], 0.0) for c in range(8)], axis=0).astype(BF16)
            )
            rows_in += [hop2_in[w * 2, 0:64, :], hop2_in[w * 2 + 1, 0:64, :]]
        vol_ref[...] += dot(jnp.concatenate(parts, axis=1), jnp.concatenate(rows_in, axis=0))
        return 0

    lax.fori_loop(0, 4, insert, 0)
    lax.fori_loop(1, 16, lambda i, _: (c_copy(i).wait_send(), 0)[1], 0)


def per_device(particles, defocus, noise_weight, projections, row_slab, row_slot, interp):
    vmem, dma = pltpu.VMEM, pltpu.SemaphoreType.DMA
    volume, class_weight = pl.pallas_call(
        kernel,
        out_shape=(jax.ShapeDtypeStruct((512, 128), F32), jax.ShapeDtypeStruct((4, 8), F32)),
        in_specs=[pl.BlockSpec(memory_space=pl.ANY)] * 7,
        out_specs=(pl.BlockSpec(memory_space=vmem), pl.BlockSpec(memory_space=vmem)),
        scratch_shapes=[
            vmem((512, 128), BF16),
            vmem((1, 4), F32),
            vmem((64, 128), F32),
            vmem((1024, 128), BF16),
            vmem((4, 128), jnp.int32),
            vmem((4, 128), jnp.int32),
            vmem((4, 128), F32),
            vmem((512, 128), F32),
            vmem((1024, 128), F32),
            vmem((128, 128), F32),
            vmem((512, 128), F32),
            vmem((8, 544, 128), BF16),
            vmem((4, 1024, 128), BF16),
            vmem((512, 128), F32),
            vmem((8, 256, 1024), BF16),
            vmem((8, 256, 1024), BF16),
            vmem((2, 256, 128), F32),
            vmem((2, 64, 128), F32),
            vmem((16, 80, 128), BF16),
            vmem((16, 80, 128), BF16),
            vmem((16, 80, 128), BF16),
            vmem((16, 80, 128), BF16),
            vmem((16, 8, 128), F32),
            vmem((16, 8, 128), F32),
            vmem((8, 128), F32),
            vmem((4, 128, 128), F32),
            dma((7,)), dma((4,)), dma((4,)), dma((4,)), dma((4,)), dma((6,)), dma((6,)), dma((16,)), dma((16,)),
            dma((16,)), dma((16,)), dma((16,)), dma((16,)), dma((16,)), dma((16,)),
        ],
        compiler_params=pltpu.CompilerParams(
            collective_id=0, has_side_effects=True, vmem_limit_bytes=56 * 1024 * 1024
        ),
    )(
        particles.reshape(512, 128), defocus.reshape(1, 4), noise_weight.T, projections.reshape(1024, 128),
        row_slab.reshape(4, 128), row_slot, interp,
    )
    return volume.reshape(8, 64, 128), class_weight


def solution(mesh):
    in_specs = (
        P(("blk", "dom"), None, None),
        P(("blk", "dom")),
        P(),
        P(None, "blk", None, None),
        P(("blk", "dom"), None, None),
        P(("blk", "dom"), None),
        P(("blk", "dom"), None),
    )
    out_specs = (P(None, ("blk", "dom"), None), P(("blk", "dom"), None))
    return jax.shard_map(per_device, mesh=mesh, in_specs=in_specs, out_specs=out_specs, check_vma=False)
```

time: 52.6 us -> 47.8 us (0.909)
  Pallas kernels: 49.6 us -> 44.8 us
    pallas_call x1, Pallas kernels: 49.6 us -> 44.8 us  [per_device(): pl.pallas_call(kernel, out_shape=(jax.ShapeDtypeStruct((512, 128), F32),...]
where the time goes in v2:
time: 47.8 us; the launch traced here: 47.7 us
  Pallas kernels  44.8 us (94%)
  local copies, waits for them, and re-layouts  2.25 us (5%)
  between operations  0.65 us (1%)
    pallas_call x1, Pallas kernels, per_device(): pl.pallas_call(kernel, out_shape=(jax.ShapeDtypeStruct((512, 128), F32),...  44.8 us
    unnamed x4, local copies, waits for them, and re-layouts  2.25 us

profile of v2, /device:TPU:1, one launch (start us, length us, event | category | flops | bytes accessed | tf_op | source)
XLA Modules:
  0.0 47.7 jit_solution(3172975296206636591)
XLA Ops:
  0.6 44.8 %shard_map.86 = (f32[512,128]{1,0:T(8,128)}, f32[4,8]{1,0:T(4,128)}) custom-call(bf16[512,128]{1,0:T(8,128)(2,1)} %bitcast.8, f32[1,4]{1,0:T(1,128)} %bitcast.11, f32[64,128]{1,0:T(8,128)} %bitcast.9, bf16[1024,128]{1,0:T(8,128)(2,1)} %bitcast.6, s32[4,128]{1,0:T(4,128)} %bitcast.10, s32[4,128]{1,0:T(4,128)} %slot_hbm.1, f32[4,128]{1,0:T(4,128)} %interp_hbm.1), custom_call_target="tpu_custom_call" | custom-call | tf_op jit(solution)/shard_map/pallas_call | solution.py:531
  45.4 0.0 copy-start
  45.4 1.7 %copy.11 = f32[8,64,128]{2,1,0:T(8,128)} copy(f32[8,64,128]{2,1,0:T(8,128)} %bitcast.7) | data formatting | bytes 524288
  47.1 0.0 copy-done
  47.1 0.6 %copy.12 = f32[4,8]{1,0:T(4,128)} copy(f32[4,8]{1,0:T(4,128)S(1)} %copy-done) | data formatting | bytes 256
Async XLA Ops:
  45.4 1.7 %copy-start = (f32[4,8]{1,0:T(4,128)S(1)}, f32[4,8]{1,0:T(4,128)}, u32[]{:S(2)}) copy-start(f32[4,8]{1,0:T(4,128)} %get-tuple-element.9) | copy-start | bytes 388

commit v3 on v2

--- a/solution.py
+++ b/solution.py
@@ -7,6 +7,7 @@
 
 F32, BF16 = jnp.float32, jnp.bfloat16
 MESH = pl.DeviceIdType.MESH
+FAR = (8, 7, 9, 6, 10, 5, 11, 4, 12, 3, 13, 2, 14, 1, 15)
 PI = 3.141592653589793
 SIN_COEF = (
     0.9999999992267364, -0.16666665898756483, 0.008333320916259667, -0.00019840515744570079,
@@ -346,6 +347,7 @@
 
     t_copy(a).wait_recv()
     turns(z)
+    m_row, m_col = iota((256, 256), 0), iota((256, 256), 1)
     came_left(0).wait_recv()
     pass_right().start()
     came_right(1).wait_recv()
@@ -357,6 +359,12 @@
         w_copy(z, relay_from * 2 + core, relay_to * 2 + core).start()
         t_copy(relay_from * 2 + core).start()
 
+    came_left(1).wait_recv()
+    views(from_left)
+
+    came_right(0).wait_recv()
+    views(from_right)
+
     by_distance = (z + 1 - 2 * (z % 2), 2 - z // 2, 3 - 3 * (z // 2))
     for source in by_distance:
 
@@ -365,13 +373,10 @@
             w_copy(source, source * 2 + core, a).wait_recv()
             t_copy(source * 2 + core).start()
 
-    came_left(1).wait_recv()
-    views(from_left)
-    came_right(0).wait_recv()
-    views(from_right)
     for source in by_distance:
         t_copy(source * 2 + 1 - core).wait_recv()
         turns(source)
+
     p_copy(4, across_x, 0, right).wait_recv()
     p_copy(5, across_x, 1, left).wait_recv()
     views(across_x)
@@ -382,7 +387,6 @@
     for h in range(2):
         score[h] = part[:, h * 128:(h + 1) * 128]
 
-    m_row, m_col = iota((256, 256), 0), iota((256, 256), 1)
     even = jnp.concatenate([score[h, pl.ds(0, 128, stride=2), :] for h in range(2)], axis=1)
     odd = jnp.concatenate([score[h, pl.ds(1, 128, stride=2), :] for h in range(2)], axis=1)
     folded = even + pltpu.roll(odd, 255, 1)
@@ -417,7 +421,7 @@
         to = column(i)
         return copy(stat.at[v], stat.at[v], s_send.at[i], s_recv.at[i], to[0], to[1])
 
-    for i in (8, 7, 9, 6, 10, 5, 11, 4, 12, 3, 13, 2, 14, 1, 15):
+    for i in FAR:
         s_copy(i).start()
 
     lax.fori_loop(1, 16, lambda i, _: (h1_copy(i).wait_recv(), 0)[1], 0)
@@ -443,7 +447,8 @@
         to = column(i)
         return copy(hop2_out.at[(v + i) % 16], hop2_in.at[v], h2_send.at[i], h2_recv.at[i], to[0], to[1])
 
-    lax.fori_loop(1, 16, lambda i, _: (h2_copy(i).start(), 0)[1], 0)
+    for i in FAR:
+        h2_copy(i).start()
     hop2_in[v] = hop2_out[v]
     for part in range(2):
         to_right(part).wait_send()
@@ -493,7 +498,12 @@
     own_source = lane32 // 4 == iota((32, 128), 0)
     slot64 = iota((64, 128), 0).astype(F32)
     repeats = [jnp.where(o_row == ((o_col % 64) // 4) * 4 + t, 1.0, 0.0).astype(BF16) for t in range(4)]
-    vol_ref[...] = jnp.zeros_like(vol_ref)
+    slots_of, which_of = [], []
+    for w in range(8):
+        tags = jnp.concatenate([hop2_in[w * 2, 64:80, :], hop2_in[w * 2 + 1, 64:80, :]], axis=0)
+        key = jnp.sum(jnp.where(own_source, dot(tags, pick_key), 0.0), axis=0, keepdims=True) - 1.0
+        slots_of.append(jnp.floor(key * 0.25))
+        which_of.append(key - 4.0 * slots_of[w])
     lax.fori_loop(1, 16, lambda i, _: (c_copy(i).wait_recv(), 0)[1], 0)
 
     gathered = [cw_in[2 * m] + cw_in[2 * m + 1] for m in range(8)]
@@ -501,28 +511,23 @@
     for t in range(4):
         coef_tab[t] = dot(table, repeats[t])
 
-    def insert(quad, _):
+    added = jnp.zeros((512, 128), F32)
+    for quad in range(4):
         parts, rows_in = [], []
         for h in range(2):
             w = quad * 2 + h
-            tags = jnp.concatenate([hop2_in[w * 2, 64:80, :], hop2_in[w * 2 + 1, 64:80, :]], axis=0)
-            key = jnp.sum(jnp.where(own_source, dot(tags, pick_key), 0.0), axis=0, keepdims=True) - 1.0
-            at_slot = jnp.floor(key * 0.25)
-            which = key - 4.0 * at_slot
             coef = jnp.zeros((8, 128), F32)
             for p in range(4):
                 rows = h * 64 + p * 8
                 both = jnp.where(half8, coef_tab[quad, rows:rows + 8, :], coef_tab[quad, rows + 32:rows + 40, :])
-                coef = jnp.where(which == float(p), both, coef)
-            hit = slot64 == at_slot
+                coef = jnp.where(which_of[w] == float(p), both, coef)
+            hit = slot64 == slots_of[w]
             parts.append(
                 jnp.concatenate([jnp.where(hit, coef[c:c + 1, :], 0.0) for c in range(8)], axis=0).astype(BF16)
             )
             rows_in += [hop2_in[w * 2, 0:64, :], hop2_in[w * 2 + 1, 0:64, :]]
-        vol_ref[...] += dot(jnp.concatenate(parts, axis=1), jnp.concatenate(rows_in, axis=0))
-        return 0
-
-    lax.fori_loop(0, 4, insert, 0)
+        added = added + dot(jnp.concatenate(parts, axis=1), jnp.concatenate(rows_in, axis=0))
+    vol_ref[...] = added
     lax.fori_loop(1, 16, lambda i, _: (c_copy(i).wait_send(), 0)[1], 0)
 
 

time: 47.8 us -> 46.2 us (0.967)
  Pallas kernels: 44.8 us -> 43.2 us
    pallas_call x1, Pallas kernels: 44.8 us -> 43.2 us  [per_device(): pl.pallas_call(kernel, out_shape=(jax.ShapeDtypeStruct((512, 128), F32),...]
where the time goes in v3:
time: 46.2 us; the launch traced here: 46.1 us
  Pallas kernels  43.2 us (94%)
  local copies, waits for them, and re-layouts  2.25 us (5%)
  between operations  0.65 us (1%)
    pallas_call x1, Pallas kernels, per_device(): pl.pallas_call(kernel, out_shape=(jax.ShapeDtypeStruct((512, 128), F32),...  43.2 us
    unnamed x4, local copies, waits for them, and re-layouts  2.25 us

profile of v3, /device:TPU:1, one launch (start us, length us, event | category | flops | bytes accessed | tf_op | source)
XLA Modules:
  0.0 46.1 jit_solution(10153878662551113959)
XLA Ops:
  0.6 43.2 %shard_map.86 = (f32[512,128]{1,0:T(8,128)}, f32[4,8]{1,0:T(4,128)}) custom-call(bf16[512,128]{1,0:T(8,128)(2,1)} %bitcast.8, f32[1,4]{1,0:T(1,128)} %bitcast.11, f32[64,128]{1,0:T(8,128)} %bitcast.9, bf16[1024,128]{1,0:T(8,128)(2,1)} %bitcast.6, s32[4,128]{1,0:T(4,128)} %bitcast.10, s32[4,128]{1,0:T(4,128)} %slot_hbm.1, f32[4,128]{1,0:T(4,128)} %interp_hbm.1), custom_call_target="tpu_custom_call" | custom-call | tf_op jit(solution)/shard_map/pallas_call | solution.py:536
  43.8 0.0 copy-start
  43.8 1.7 %copy.11 = f32[8,64,128]{2,1,0:T(8,128)} copy(f32[8,64,128]{2,1,0:T(8,128)} %bitcast.7) | data formatting | bytes 524288
  45.5 0.0 copy-done
  45.5 0.6 %copy.12 = f32[4,8]{1,0:T(4,128)} copy(f32[4,8]{1,0:T(4,128)S(1)} %copy-done) | data formatting | bytes 256
Async XLA Ops:
  43.8 1.7 %copy-start = (f32[4,8]{1,0:T(4,128)S(1)}, f32[4,8]{1,0:T(4,128)}, u32[]{:S(2)}) copy-start(f32[4,8]{1,0:T(4,128)} %get-tuple-element.9) | copy-start | bytes 388

commit v4 on v3

--- a/solution.py
+++ b/solution.py
@@ -116,8 +116,8 @@
 
     right, left = ((x + 1) % 4) * 8 + a, ((x + 3) % 4) * 8 + a
     from_left, from_right, across_x = (x + 3) % 4, (x + 1) % 4, (x + 2) % 4
+    lax.fori_loop(1, 16, greet(plane), 0)
     lax.fori_loop(1, 16, greet(column), 0)
-    lax.fori_loop(1, 16, greet(plane), 0)
 
     def p_copy(k, block, part, to):
         rows = pl.ds(part * 512, 512)
@@ -213,6 +213,14 @@
     fetches[4].wait()
     wide_x[...] = proj_ref[...].astype(F32)
     lax.fori_loop(0, 64, order_proj, 0, unroll=8)
+
+    pl.semaphore_wait(barrier, 30)
+    each_z(lambda target: w_copy(target, a, target * 2 + core).start())
+    t_copy(a).start()
+    to_right(0).start()
+    to_left(1).start()
+    to_right(1).start()
+    to_left(0).start()
 
     fetches[5].wait()
     fetches[6].wait()
@@ -254,14 +262,6 @@
         return 0
 
     lax.fori_loop(0, 8, dispatch, 0, unroll=2)
-
-    pl.semaphore_wait(barrier, 30)
-    each_z(lambda target: w_copy(target, a, target * 2 + core).start())
-    t_copy(a).start()
-    to_right(0).start()
-    to_left(1).start()
-    to_right(1).start()
-    to_left(0).start()
 
     def h1_copy(i):
         to = plane(i)

time: 46.2 us -> 45.8 us (level)
  no operation moved by 1% of the time
where the time goes in v4:
time: 45.8 us; the launch traced here: 45.7 us
  Pallas kernels  42.8 us (93%)
  local copies, waits for them, and re-layouts  2.25 us (5%)
  between operations  0.65 us (1%)
    pallas_call x1, Pallas kernels, per_device(): pl.pallas_call(kernel, out_shape=(jax.ShapeDtypeStruct((512, 128), F32),...  42.8 us
    unnamed x4, local copies, waits for them, and re-layouts  2.25 us

profile of v4, /device:TPU:1, one launch (start us, length us, event | category | flops | bytes accessed | tf_op | source)
XLA Modules:
  0.0 45.7 jit_solution(2357690057954328598)
XLA Ops:
  0.6 42.8 %shard_map.86 = (f32[512,128]{1,0:T(8,128)}, f32[4,8]{1,0:T(4,128)}) custom-call(bf16[512,128]{1,0:T(8,128)(2,1)} %bitcast.8, f32[1,4]{1,0:T(1,128)} %bitcast.11, f32[64,128]{1,0:T(8,128)} %bitcast.9, bf16[1024,128]{1,0:T(8,128)(2,1)} %bitcast.6, s32[4,128]{1,0:T(4,128)} %bitcast.10, s32[4,128]{1,0:T(4,128)} %slot_hbm.1, f32[4,128]{1,0:T(4,128)} %interp_hbm.1), custom_call_target="tpu_custom_call" | custom-call | tf_op jit(solution)/shard_map/pallas_call | solution.py:536
  43.4 0.0 copy-start
  43.4 1.7 %copy.11 = f32[8,64,128]{2,1,0:T(8,128)} copy(f32[8,64,128]{2,1,0:T(8,128)} %bitcast.7) | data formatting | bytes 524288
  45.1 0.0 copy-done
  45.1 0.6 %copy.12 = f32[4,8]{1,0:T(4,128)} copy(f32[4,8]{1,0:T(4,128)S(1)} %copy-done) | data formatting | bytes 256
Async XLA Ops:
  43.4 1.7 %copy-start = (f32[4,8]{1,0:T(4,128)S(1)}, f32[4,8]{1,0:T(4,128)}, u32[]{:S(2)}) copy-start(f32[4,8]{1,0:T(4,128)} %get-tuple-element.9) | copy-start | bytes 388
